TPU v7x, 256 devices: a whole 4x4x8 slice. The times are simulated.
256 devices in a mesh: section: 8 (over z), et: 32 (over x, y, core).
Axes of the slice: x: 4, y: 4, z: 8, core: 2. Of those that a mesh axis runs over, the one named last changes fastest.
Arguments:
- acts: bfloat16 [8, 512, 6144], P('section', 'et'), may hold values from -6 to 6
- norm_gain: float32 [8, 6144], P('section'), may hold values from 0.5 to 1.5
- router: bfloat16 [8, 6144, 8], P('section'), may hold values from -0.078125 to 0.078125
- w_gate: bfloat16 [8, 6144, 8192], P('section', None, 'et'), may hold values from -0.078125 to 0.078125
- w_up: bfloat16 [8, 6144, 8192], P('section', None, 'et'), may hold values from -0.078125 to 0.078125
- w_down: bfloat16 [8, 8192, 6144], P('section', 'et'), may hold values from -0.0625 to 0.0625
- expert_ids: int32 [8, 8, 512, 2], P('section', None, 'et'), may hold values from 0 to 7, as said below
Outputs:
- finished: bfloat16 [8, 512, 6144], P('section', 'et')
Inputs may be any that keep to these rules, and one draw needn't show every extreme that they name: `expert_ids`: the two ids of a row differ. Of the 16 rows of one device in one micro-batch and layer, 1 to 4 name expert 0; for each layer, one micro-batch has exactly 4 such rows on every device.
All inputs are finite; a program needn't handle non-finite values.
Results may differ from a plain program's by a relative error of at most 0.014.
Values may be sent and summed in bfloat16 or wider, within the bound.
A program may use at most 64 MiB of HBM per device.

v0:
```python
import jax
import jax.numpy as jnp
from jax import lax
from jax.sharding import PartitionSpec as P


def shifted(x, axis, by):
    devices = lax.axis_size(axis)
    return lax.ppermute(x, axis, [(i, (i + by) % devices) for i in range(devices)])


def expert_layer(current, gain, router, w_gate, w_up, w_down, routing):
    rows = current.shape[0]
    capacity = rows // 4
    xf = current.astype(jnp.float32)
    scale = lax.rsqrt(jnp.mean(xf * xf, axis=-1, keepdims=True) + 1e-05)
    normed = (xf * scale * gain).astype(jnp.bfloat16)
    logits = jnp.dot(normed, router, preferred_element_type=jnp.float32)
    columns = jnp.arange(router.shape[1], dtype=jnp.int32)
    first = routing[:, 0]
    second = routing[:, 1]
    l_first = jnp.sum(jnp.where(columns[None, :] == first[:, None], logits, 0.0), axis=-1)
    l_second = jnp.sum(jnp.where(columns[None, :] == second[:, None], logits, 0.0), axis=-1)
    held = (first == 0) | (second == 0)
    rival = jnp.where(first == 0, l_second, l_first)
    gate = jnp.where(held, jax.nn.sigmoid(logits[:, 0] - rival), jnp.float32(0.0))
    position = jnp.cumsum(held.astype(jnp.int32)) - 1
    slot_ids = jnp.arange(capacity, dtype=jnp.int32)
    select = held[None, :] & (position[None, :] == slot_ids[:, None])
    slots = jnp.dot(select.astype(jnp.bfloat16), normed, preferred_element_type=jnp.float32).astype(
        jnp.bfloat16
    )
    piece = lax.all_gather(slots, "et", axis=0, tiled=True)
    gate_part = jnp.dot(piece, w_gate, preferred_element_type=jnp.float32)
    up_part = jnp.dot(piece, w_up, preferred_element_type=jnp.float32)
    hidden = (jax.nn.silu(gate_part) * up_part).astype(jnp.bfloat16)
    expert_out = lax.psum_scatter(
        jnp.dot(hidden, w_down, preferred_element_type=jnp.float32).astype(jnp.bfloat16),
        "et",
        scatter_dimension=0,
        tiled=True,
    ).astype(jnp.float32)
    back = jnp.dot(select.astype(jnp.float32).T, expert_out, precision=lax.Precision.HIGHEST)
    return (xf + gate[:, None] * back).astype(jnp.bfloat16)


def body(acts, norm_gain, router, w_gate, w_up, w_down, expert_ids):
    sections = lax.axis_size("section")
    position = lax.axis_index("section")
    current = acts[0]
    for turn_number in range(sections):
        held_batch = (position - turn_number) % sections
        routing = lax.dynamic_index_in_dim(expert_ids[0], held_batch, 0, keepdims=False)
        current = jnp.where(
            turn_number <= position,
            expert_layer(current, norm_gain[0], router[0], w_gate[0], w_up[0], w_down[0], routing),
            current,
        )
        current = shifted(current, "section", 1)
    return current[None]


def solution(mesh):
    return jax.shard_map(
        body,
        mesh=mesh,
        in_specs=(
            P("section", "et", None),
            P("section", None),
            P("section", None, None),
            P("section", None, "et"),
            P("section", None, "et"),
            P("section", "et", None),
            P("section", None, "et", None),
        ),
        out_specs=P("section", "et", None),
        check_vma=False,
    )
```

profile of v0, /device:TPU:6, one launch (start us, length us, event | category | flops | bytes accessed | tf_op | source)
XLA Modules:
  0.0 1510.1 jit_solution(235335633677862347)
XLA Ops:
  7.5 1.2 fusion.136
  8.9 1.8 fusion.24
  10.9 1.3 dynamic-slice.8
  12.8 48.9 %all-gather.17.cloned.1.call-done = bf16[32,4,6144]{2,1,0:T(4,128)(2,1)} async-done(((bf16[1,4,6144]{2,1,0:T(4,128)(2,1)}), bf16[32,4,6144]{2,1,0:T(4,128)(2,1)}) %all-gather.17.cloned.1.call-update) | async-done | bytes 1572880 | tf_op jit(solution)/shard_map/all_gather | solution.py:33
  61.7 3.6 reshape.375
  65.4 2.9 fusion.70
  68.3 5.4 convolution_convert_fusion.7
  75.0 115.7 %all-reduce.17.cloned.1.call-done = bf16[128,6144]{1,0:T(8,128)(2,1)} async-done(((bf16[128,6144]{1,0:T(8,128)(2,1)}), bf16[128,6144]{1,0:T(8,128)(2,1)}) %all-reduce.17.cloned.1.call-update) | async-done | bytes 1572880
  191.9 1.6 collective-permute-start
  193.5 5.4 collective-permute-done
  200.2 47.8 %all-gather.19.cloned.1.call-done = bf16[32,4,6144]{2,1,0:T(4,128)(2,1)} async-done(((bf16[1,4,6144]{2,1,0:T(4,128)(2,1)}), bf16[32,4,6144]{2,1,0:T(4,128)(2,1)}) %all-gather.19.cloned.1.call-update) | async-done | bytes 1572880 | tf_op jit(solution)/shard_map/all_gather | solution.py:33
  248.0 3.7 reshape.377
  251.7 2.9 fusion.68
  254.6 5.4 convolution_convert_fusion.6
  261.2 115.8 %all-reduce.19.cloned.1.call-done = bf16[128,6144]{1,0:T(8,128)(2,1)} async-done(((bf16[128,6144]{1,0:T(8,128)(2,1)}), bf16[128,6144]{1,0:T(8,128)(2,1)}) %all-reduce.19.cloned.1.call-update) | async-done | bytes 1572880
  378.1 1.6 collective-permute-start.1
  379.8 5.4 collective-permute-done.1
  386.6 47.6 %all-gather.21.cloned.1.call-done = bf16[32,4,6144]{2,1,0:T(4,128)(2,1)} async-done(((bf16[1,4,6144]{2,1,0:T(4,128)(2,1)}), bf16[32,4,6144]{2,1,0:T(4,128)(2,1)}) %all-gather.21.cloned.1.call-update) | async-done | bytes 1572880 | tf_op jit(solution)/shard_map/all_gather | solution.py:33
  434.3 3.7 reshape.379
  437.9 2.9 fusion.66
  440.9 5.4 convolution_convert_fusion.5
  447.4 115.8 %all-reduce.21.cloned.1.call-done = bf16[128,6144]{1,0:T(8,128)(2,1)} async-done(((bf16[128,6144]{1,0:T(8,128)(2,1)}), bf16[128,6144]{1,0:T(8,128)(2,1)}) %all-reduce.21.cloned.1.call-update) | async-done | bytes 1572880
  563.2 1.2 fusion.21
  564.4 1.6 collective-permute-start.2
  566.1 5.4 collective-permute-done.2
  572.7 47.8 %all-gather.23.cloned.1.call-done = bf16[32,4,6144]{2,1,0:T(4,128)(2,1)} async-done(((bf16[1,4,6144]{2,1,0:T(4,128)(2,1)}), bf16[32,4,6144]{2,1,0:T(4,128)(2,1)}) %all-gather.23.cloned.1.call-update) | async-done | bytes 1572880 | tf_op jit(solution)/shard_map/all_gather | solution.py:33
  620.5 3.7 reshape.381
  624.2 2.9 fusion.64
  627.1 5.4 convolution_convert_fusion.4
  633.7 115.8 %all-reduce.23.cloned.1.call-done = bf16[128,6144]{1,0:T(8,128)(2,1)} async-done(((bf16[128,6144]{1,0:T(8,128)(2,1)}), bf16[128,6144]{1,0:T(8,128)(2,1)}) %all-reduce.23.cloned.1.call-update) | async-done | bytes 1572880
  750.7 1.6 collective-permute-start.3
  752.3 5.4 collective-permute-done.3
  759.0 47.8 %all-gather.25.cloned.1.call-done = bf16[32,4,6144]{2,1,0:T(4,128)(2,1)} async-done(((bf16[1,4,6144]{2,1,0:T(4,128)(2,1)}), bf16[32,4,6144]{2,1,0:T(4,128)(2,1)}) %all-gather.25.cloned.1.call-update) | async-done | bytes 1572880 | tf_op jit(solution)/shard_map/all_gather | solution.py:33
  806.8 3.7 reshape.383
  810.5 2.9 fusion.62
  813.4 5.4 convolution_convert_fusion.3
  820.0 115.8 %all-reduce.25.cloned.1.call-done = bf16[128,6144]{1,0:T(8,128)(2,1)} async-done(((bf16[128,6144]{1,0:T(8,128)(2,1)}), bf16[128,6144]{1,0:T(8,128)(2,1)}) %all-reduce.25.cloned.1.call-update) | async-done | bytes 1572880
  935.7 1.2 fusion.19
  936.9 1.9 collective-permute-start.4
  938.8 5.4 collective-permute-done.4
  945.4 47.8 %all-gather.27.cloned.1.call-done = bf16[32,4,6144]{2,1,0:T(4,128)(2,1)} async-done(((bf16[1,4,6144]{2,1,0:T(4,128)(2,1)}), bf16[32,4,6144]{2,1,0:T(4,128)(2,1)}) %all-gather.27.cloned.1.call-update) | async-done | bytes 1572880 | tf_op jit(solution)/shard_map/all_gather | solution.py:33
  993.2 3.7 reshape.385
  996.9 2.9 fusion.60
  999.9 5.4 convolution_convert_fusion.2
  1006.4 115.8 %all-reduce.27.cloned.1.call-done = bf16[128,6144]{1,0:T(8,128)(2,1)} async-done(((bf16[128,6144]{1,0:T(8,128)(2,1)}), bf16[128,6144]{1,0:T(8,128)(2,1)}) %all-reduce.27.cloned.1.call-update) | async-done | bytes 1572880
  1122.2 1.2 fusion.18
  1123.4 1.6 collective-permute-start.5
  1125.0 5.4 collective-permute-done.5
  1131.7 47.8 %all-gather.29.cloned.1.call-done = bf16[32,4,6144]{2,1,0:T(4,128)(2,1)} async-done(((bf16[1,4,6144]{2,1,0:T(4,128)(2,1)}), bf16[32,4,6144]{2,1,0:T(4,128)(2,1)}) %all-gather.29.cloned.1.call-update) | async-done | bytes 1572880 | tf_op jit(solution)/shard_map/all_gather | solution.py:33
  1179.5 3.7 reshape.387
  1183.1 2.9 fusion.58
  1186.1 5.4 convolution_convert_fusion.1
  1192.6 115.8 %all-reduce.29.cloned.1.call-done = bf16[128,6144]{1,0:T(8,128)(2,1)} async-done(((bf16[128,6144]{1,0:T(8,128)(2,1)}), bf16[128,6144]{1,0:T(8,128)(2,1)}) %all-reduce.29.cloned.1.call-update) | async-done | bytes 1572880
  1308.4 1.2 fusion.17
  1309.6 1.6 collective-permute-start.6
  1311.2 5.4 collective-permute-done.6
  1317.8 48.0 %all-gather.31.cloned.1.call-done = bf16[32,4,6144]{2,1,0:T(4,128)(2,1)} async-done(((bf16[1,4,6144]{2,1,0:T(4,128)(2,1)}), bf16[32,4,6144]{2,1,0:T(4,128)(2,1)}) %all-gather.31.cloned.1.call-update) | async-done | bytes 1572880 | tf_op jit(solution)/shard_map/all_gather | solution.py:33
  1365.7 3.7 reshape.389
  1369.4 2.9 fusion.56
  1372.3 5.4 convolution_convert_fusion
  1378.9 115.8 %all-reduce.31.cloned.1.call-done = bf16[128,6144]{1,0:T(8,128)(2,1)} async-done(((bf16[128,6144]{1,0:T(8,128)(2,1)}), bf16[128,6144]{1,0:T(8,128)(2,1)}) %all-reduce.31.cloned.1.call-update) | async-done | bytes 1572880
  1494.7 1.2 fusion.16
  1495.9 1.6 collective-permute-start.7
  1497.5 5.4 collective-permute-done.7
  (145 shorter events, 23.6 us)
Async XLA Ops:
  6.5 61.8 %copy-start = (bf16[1,256,6144]{2,1,0:T(8,128)(2,1)S(1)}, bf16[1,256,6144]{2,1,0:T(8,128)(2,1)}, u32[]{:S(2)}) copy-start(bf16[1,256,6144]{2,1,0:T(8,128)(2,1)} %param.12) | copy-start | bytes 9437188
  6.5 55.2 %all-gather.17.cloned.1.call-start = ((), (), s32[]{:S(2)}) async-start(), calls=%async_computation | async-start | bytes 1622016 | tf_op jit(solution)/shard_map/all_gather | solution.py:33
  10.7 180.0 %all-reduce.17.cloned.1.call-start = ((), (), s32[]{:S(2)}) async-start(), calls=%async_computation.8 | async-start | bytes 3145728
  73.7 0.9 copy-start.1
  73.7 1.0 copy-start.2
  73.7 1.0 copy-start.10
  73.8 174.2 %all-gather.19.cloned.1.call-start = ((), (), s32[]{:S(2)}) async-start(), calls=%async_computation.1 | async-start | bytes 1622016 | tf_op jit(solution)/shard_map/all_gather | solution.py:33
  191.9 7.0 collective-permute-start
  200.0 177.0 %all-reduce.19.cloned.1.call-start = ((), (), s32[]{:S(2)}) async-start(), calls=%async_computation.9 | async-start | bytes 3145728
  260.0 0.9 copy-start.3
  260.0 174.2 %all-gather.21.cloned.1.call-start = ((), (), s32[]{:S(2)}) async-start(), calls=%async_computation.2 | async-start | bytes 1622016 | tf_op jit(solution)/shard_map/all_gather | solution.py:33
  378.1 7.0 collective-permute-start.1
  386.3 177.0 %all-reduce.21.cloned.1.call-start = ((), (), s32[]{:S(2)}) async-start(), calls=%async_computation.10 | async-start | bytes 3145728
  446.2 0.9 copy-start.4
  446.3 174.3 %all-gather.23.cloned.1.call-start = ((), (), s32[]{:S(2)}) async-start(), calls=%async_computation.3 | async-start | bytes 1622016 | tf_op jit(solution)/shard_map/all_gather | solution.py:33
  564.4 7.0 collective-permute-start.2
  572.5 177.0 %all-reduce.23.cloned.1.call-start = ((), (), s32[]{:S(2)}) async-start(), calls=%async_computation.11 | async-start | bytes 3145728
  632.5 0.9 copy-start.5
  632.5 174.2 %all-gather.25.cloned.1.call-start = ((), (), s32[]{:S(2)}) async-start(), calls=%async_computation.4 | async-start | bytes 1622016 | tf_op jit(solution)/shard_map/all_gather | solution.py:33
  750.7 7.0 collective-permute-start.3
  758.8 177.0 %all-reduce.25.cloned.1.call-start = ((), (), s32[]{:S(2)}) async-start(), calls=%async_computation.12 | async-start | bytes 3145728
  818.8 0.9 copy-start.6
  818.8 174.4 %all-gather.27.cloned.1.call-start = ((), (), s32[]{:S(2)}) async-start(), calls=%async_computation.5 | async-start | bytes 1622016 | tf_op jit(solution)/shard_map/all_gather | solution.py:33
  936.9 7.3 collective-permute-start.4
  945.2 177.0 %all-reduce.27.cloned.1.call-start = ((), (), s32[]{:S(2)}) async-start(), calls=%async_computation.13 | async-start | bytes 3145728
  1005.2 0.9 copy-start.7
  1005.3 174.2 %all-gather.29.cloned.1.call-start = ((), (), s32[]{:S(2)}) async-start(), calls=%async_computation.6 | async-start | bytes 1622016 | tf_op jit(solution)/shard_map/all_gather | solution.py:33
  1123.4 7.0 collective-permute-start.5
  1131.5 177.0 %all-reduce.29.cloned.1.call-start = ((), (), s32[]{:S(2)}) async-start(), calls=%async_computation.14 | async-start | bytes 3145728
  1191.5 0.9 copy-start.8
  1191.5 174.2 %all-gather.31.cloned.1.call-start = ((), (), s32[]{:S(2)}) async-start(), calls=%async_computation.7 | async-start | bytes 1622016 | tf_op jit(solution)/shard_map/all_gather | solution.py:33
  1309.6 7.0 collective-permute-start.6
  1317.7 177.0 %all-reduce.31.cloned.1.call-start = ((), (), s32[]{:S(2)}) async-start(), calls=%async_computation.15 | async-start | bytes 3145728
  1377.7 0.9 copy-start.9
  1495.9 7.0 collective-permute-start.7
Sparse Core Ops, SparseCore 0:
  10.9 50.8 all-gather.16
  73.9 116.7 all-reduce.16
  200.1 47.8 all-gather.18
  260.1 116.7 all-reduce.18
  386.4 47.8 all-gather.20
  446.4 116.8 all-reduce.20
  572.6 47.8 all-gather.22
  632.7 116.7 all-reduce.22
  758.9 47.8 all-gather.24
  818.9 116.7 all-reduce.24
  945.4 47.8 all-gather.26
  1005.4 116.7 all-reduce.26
  1131.6 47.8 all-gather.28
  1191.6 116.7 all-reduce.28
  1317.8 47.8 all-gather.30
  1377.9 116.7 all-reduce.30
where the time goes:
time: 1510 us
  waiting for transfers between devices  1350 us (89%)
  matrix products  85.8 us (6%)
  local copies, waits for them, and re-layouts  38.7 us (3%)
    unnamed x24, waiting for transfers between devices  927 us
    all_gather x8, waiting for transfers between devices, expert_layer(): piece = lax.all_gather(slots, 'et', axis=0, tiled=True)  384 us
    ppermute x8, waiting for transfers between devices, shifted(): lax.ppermute(x, axis, [(i, (i + by) % devices) for i in range(devices)])  43.2 us
    dot_general x8, matrix products, expert_layer(): jnp.dot(hidden, w_down, preferred_element_type=jnp.float32)  43 us
    unnamed x32, local copies, waits for them, and re-layouts  37.1 us
  transfers between devices with their start and end apart: 24, of which 24 were waited for; matrix products, arithmetic and copies ran while one was open for 0% of the time, Pallas kernels for 0%

commit v1 on v0

v1 whole, which is shorter than its diff:
```python
import functools
import math

import jax
import jax.numpy as jnp
from jax import lax
from jax.experimental import pallas as pl
from jax.experimental.pallas import tpu as pltpu
from jax.sharding import PartitionSpec as P

MESH = pl.DeviceIdType.MESH
F32 = jnp.float32
BF16 = jnp.bfloat16
CAP = 4
FOLD = 4
EPS = 1e-05


def iota(shape, dim):
    return lax.broadcasted_iota(jnp.int32, shape, dim)


def contract(a, b, dim_a, dim_b):
    return lax.dot_general(a, b, (((dim_a,), (dim_b,)), ((), ())), preferred_element_type=F32)


def relay_kernel(
    sections, side, acts, gain, router, w_gate, w_up, w_down, ids, out,
    wg, wu, wd, gathered, terms, landed, rows, chosen, early_out, early_in, late_out, late_in,
    xg, spread, perm, grow, gain_fold, next_route, next_pre, gates,
    w_local, w_send, w_recv, ag_send, ag_recv, rs_send, rs_recv, z_send, z_recv, credit,
):
    chips = side * side
    n_rows, depth = acts.shape[1], acts.shape[2]
    width = depth // FOLD
    hid = w_down.shape[1]
    lanes = FOLD * n_rows
    block = FOLD * CAP
    total = chips * block
    taken = chips * CAP

    section = lax.axis_index("section")
    et = lax.axis_index("et")
    core = lax.rem(et, 2)
    chip = et // 2
    cx = chip // side
    cy = lax.rem(chip, side)

    offsets = [(dx, dy) for dx in range(side) for dy in range(side) if dx or dy]
    offsets.sort(key=lambda o: -(min(o[0], side - o[0]) + min(o[1], side - o[1])))
    peers = []
    for dx, dy in offsets:
        there = lax.rem(cx + dx, side) * side + lax.rem(cy + dy, side)
        peers.append((there, (section, there * 2 + core)))
    sibling = (section, chip * 2 + 1 - core)
    above = (lax.rem(section + 1, sections), et)
    below = (lax.rem(section + sections - 1, sections), et)

    barrier = pltpu.get_barrier_semaphore()
    partners = [d for _, d in peers] + [sibling, above, below]
    for device in partners:
        pl.semaphore_signal(barrier, inc=1, device_id=device, device_id_type=MESH)

    loads = [
        pltpu.make_async_copy(src.at[0], dst.at[0], w_local.at[i])
        for i, (src, dst) in enumerate(((w_gate, wg), (w_up, wu), (w_down, wd)))
    ]
    for load in loads:
        load.start()

    def routing(turn):
        batch = lax.rem(section - turn + 2 * sections, sections)
        both = ids[0, batch].astype(F32)
        first, second = both[:, 0:1], both[:, 1:2]
        held = jnp.where((first == 0.0) | (second == 0.0), 1.0, 0.0) * (turn <= section).astype(F32)
        other = (first + second) * held
        row = iota((n_rows, lanes), 0)
        lane_row = lax.rem(iota((n_rows, lanes), 1), n_rows)
        same = row == lane_row
        held_lane = jnp.sum(jnp.where(same, held, 0.0), axis=0, keepdims=True)
        other_lane = jnp.sum(jnp.where(same, other, 0.0), axis=0, keepdims=True)
        place = jnp.sum(jnp.where(row <= lane_row, held, 0.0), axis=0, keepdims=True) - 1.0
        i = iota((block, lanes), 0)
        j = iota((block, lanes), 1)
        match = (i // CAP == j // n_rows) & (lax.rem(i, CAP).astype(F32) == place) & (held_lane > 0.0)
        select = jnp.where(match, 1.0, 0.0)
        rival = jnp.sum(select * other_lane, axis=1, keepdims=True)
        valid = jnp.sum(select, axis=1, keepdims=True)
        diag = iota((lanes, lanes), 0) == iota((lanes, lanes), 1)
        keep = jnp.where(diag & (held_lane == 0.0), 1.0, 0.0).astype(BF16)
        return select.astype(BF16), rival, valid, keep

    i = iota((total, total), 0)
    j = iota((total, total), 1)
    source = lax.rem(i, taken) // CAP * block + i // taken * CAP + lax.rem(i, CAP)
    perm[...] = jnp.where(j == source, 1.0, 0.0).astype(BF16)
    i = iota((total, taken), 0)
    j = iota((total, taken), 1)
    grow[...] = jnp.where(j == i // block * CAP + lax.rem(i, CAP), 1.0, 0.0).astype(BF16)
    fold_of = iota((block, 1), 0) // CAP
    folded = jnp.zeros((block, width), F32)
    for a in range(FOLD):
        folded = jnp.where(fold_of == a, gain[0:1, a * width : (a + 1) * width], folded)
    gain_fold[...] = folded

    for a in range(FOLD):
        rows[a * n_rows : (a + 1) * n_rows, :] = acts[0, :, a * width : (a + 1) * width]
    select, _, _, _ = routing(0)
    chosen[...] = jnp.dot(select, rows[...], preferred_element_type=F32).astype(BF16)
    gathered[chip] = chosen[...]

    pl.semaphore_wait(barrier, len(partners))

    gather = [
        pltpu.make_async_remote_copy(
            src_ref=chosen, dst_ref=gathered.at[chip], send_sem=ag_send.at[n], recv_sem=ag_recv.at[n],
            device_id=device, device_id_type=MESH,
        )
        for n, (_, device) in enumerate(peers)
    ]
    scatter = [
        pltpu.make_async_remote_copy(
            src_ref=terms.at[there], dst_ref=landed.at[chip], send_sem=rs_send.at[n], recv_sem=rs_recv.at[n],
            device_id=device, device_id_type=MESH,
        )
        for n, (there, device) in enumerate(peers)
    ]
    early = pltpu.make_async_remote_copy(
        src_ref=early_out, dst_ref=early_in, send_sem=z_send.at[0], recv_sem=z_recv.at[0],
        device_id=above, device_id_type=MESH,
    )
    late = pltpu.make_async_remote_copy(
        src_ref=late_out, dst_ref=late_in, send_sem=z_send.at[1], recv_sem=z_recv.at[1],
        device_id=above, device_id_type=MESH,
    )
    for copy in gather:
        copy.start()
    swaps = [
        pltpu.make_async_remote_copy(
            src_ref=src.at[0], dst_ref=dst.at[1], send_sem=w_send.at[i], recv_sem=w_recv.at[i],
            device_id=sibling, device_id_type=MESH,
        )
        for i, (src, dst) in enumerate(((w_gate, wg), (w_up, wu), (w_down, wd)))
    ]
    for swap in swaps:
        swap.start()

    def merged():
        incoming = contract(early_in[lanes : lanes + block, 0:lanes], late_in[...], 0, 0)
        return (early_in[0:lanes, :].astype(F32) + incoming).astype(BF16)

    def turn_body(turn, carry):
        @pl.when(turn > 0)
        def _():
            rows[...] = merged()
            pl.semaphore_signal(credit, inc=1, device_id=below, device_id_type=MESH)

        select, rival, valid, keep = routing(turn)

        @pl.when(turn > 0)
        def _():
            early.wait_send()
            late.wait_send()

        early_out[0:lanes, :] = jnp.dot(keep, rows[...], preferred_element_type=F32).astype(BF16)
        early_out[lanes : lanes + block, 0:lanes] = select

        @pl.when(turn > 0)
        def _():
            pl.semaphore_wait(credit, 1)

        early.start()

        x = chosen[...].astype(F32)
        weighted = (x * gain_fold[...]).astype(BF16)
        partial = jnp.zeros((block, router.shape[2]), F32)
        for a in range(FOLD):
            part = jnp.dot(weighted, router[0, a * width : (a + 1) * width, :], preferred_element_type=F32)
            partial = jnp.where(fold_of == a, part, partial)
        square = jnp.sum(x * x, axis=1, keepdims=True)
        logits = jnp.zeros_like(partial)
        squares = jnp.zeros_like(square)
        row_slot = lax.rem(iota((block, 1), 0), CAP)
        for slot in range(CAP):
            here = row_slot == slot
            logits = jnp.where(here, jnp.sum(jnp.where(here, partial, 0.0), axis=0, keepdims=True), logits)
            squares = jnp.where(here, jnp.sum(jnp.where(here, square, 0.0), axis=0, keepdims=True), squares)
        logits = logits * lax.rsqrt(squares / depth + EPS)
        expert = iota(logits.shape, 1).astype(F32)
        l_rival = jnp.sum(jnp.where(expert == rival, logits, 0.0), axis=1, keepdims=True)
        gates[...] = jnp.broadcast_to(valid * jax.nn.sigmoid(logits[:, 0:1] - l_rival), gates.shape)

        for copy in reversed(gather):
            copy.wait_recv()
        everyone = gathered[...].reshape(total, width)
        ordered = jnp.dot(perm[...], everyone, preferred_element_type=F32)
        square = jnp.zeros((taken, 1), F32)
        for a in range(FOLD):
            piece = ordered[a * taken : (a + 1) * taken, :]
            square = square + jnp.sum(piece * piece, axis=1, keepdims=True)
            xg[:, a * width : (a + 1) * width] = (piece * gain[0:1, a * width : (a + 1) * width]).astype(BF16)
        scale = lax.rsqrt(square / depth + EPS)

        @pl.when(turn == 0)
        def _():
            for copy in loads[:2]:
                copy.wait()
            for copy in swaps[:2]:
                copy.wait()

        hidden = []
        for half in range(2):
            g = jnp.dot(xg[...], wg[half], preferred_element_type=F32) * scale
            u = jnp.dot(xg[...], wu[half], preferred_element_type=F32) * scale
            hidden.append((jax.nn.silu(g) * u).astype(BF16))
        row_fold = lax.rem(iota((total, hid), 0), block) // CAP
        for half in range(2):
            wide = jnp.dot(grow[...], hidden[half], preferred_element_type=F32)
            for a in range(FOLD):
                spread[:, (a * 2 + half) * hid : (a * 2 + half + 1) * hid] = jnp.where(
                    row_fold == a, wide, 0.0
                ).astype(BF16)

        @pl.when(turn == 0)
        def _():
            loads[2].wait()
            swaps[2].wait()

        step = math.gcd(width, 256)
        for n in range(0, width, step):
            acc = jnp.zeros((total, step), F32)
            for a in range(FOLD):
                for half in range(2):
                    acc = acc + jnp.dot(
                        spread[:, (a * 2 + half) * hid : (a * 2 + half + 1) * hid],
                        wd[half, :, a * width + n : a * width + n + step],
                        preferred_element_type=F32,
                    )
            terms[:, :, n : n + step] = acc.astype(BF16).reshape(chips, block, step)
        for copy in scatter:
            copy.start()

        landed[chip] = terms[chip]
        for copy in gather:
            copy.wait_send()
        early.wait_recv()
        ahead, _, _, _ = routing(turn + 1)
        next_pre[...] = jnp.dot(ahead, early_in[0:lanes, :], preferred_element_type=F32)
        next_route[...] = contract(ahead, early_in[lanes : lanes + block, 0:lanes], 1, 1).astype(BF16)

        for copy in reversed(scatter):
            copy.wait_recv()
        sums = landed[0].astype(F32)
        for source_chip in range(1, chips):
            sums = sums + landed[source_chip].astype(F32)
        late_out[...] = (chosen[...].astype(F32) + gates[:, 0:1] * sums).astype(BF16)
        late.start()
        for copy in scatter:
            copy.wait_send()
        late.wait_recv()
        picked = next_pre[...] + jnp.dot(next_route[...], late_in[...], preferred_element_type=F32)

        @pl.when(turn < sections - 1)
        def _():
            chosen[...] = picked.astype(BF16)
            for copy in gather:
                copy.start()
            gathered[chip] = chosen[...]

        return carry

    lax.fori_loop(0, sections, turn_body, 0)

    final = merged()
    for a in range(FOLD):
        out[0, :, a * width : (a + 1) * width] = final[a * n_rows : (a + 1) * n_rows, :]
    early.wait_send()
    late.wait_send()


def body(sections, side, acts, norm_gain, router, w_gate, w_up, w_down, expert_ids):
    chips = side * side
    n_rows, depth = acts.shape[1], acts.shape[2]
    width = depth // FOLD
    hid = w_gate.shape[2]
    lanes = FOLD * n_rows
    block = FOLD * CAP
    total = chips * block
    taken = chips * CAP
    peers = chips - 1
    vmem = pl.BlockSpec(memory_space=pltpu.VMEM)
    hbm = pl.BlockSpec(memory_space=pl.ANY)
    dma = pltpu.SemaphoreType.DMA
    return pl.pallas_call(
        functools.partial(relay_kernel, sections, side),
        out_shape=jax.ShapeDtypeStruct(acts.shape, acts.dtype),
        in_specs=[vmem, vmem, vmem, hbm, hbm, hbm, vmem],
        out_specs=vmem,
        scratch_shapes=[
            pltpu.VMEM((2, depth, hid), BF16),
            pltpu.VMEM((2, depth, hid), BF16),
            pltpu.VMEM((2, hid, depth), BF16),
            pltpu.VMEM((chips, block, width), BF16),
            pltpu.VMEM((chips, block, width), BF16),
            pltpu.VMEM((chips, block, width), BF16),
            pltpu.VMEM((lanes, width), BF16),
            pltpu.VMEM((block, width), BF16),
            pltpu.VMEM((lanes + block, width), BF16),
            pltpu.VMEM((lanes + block, width), BF16),
            pltpu.VMEM((block, width), BF16),
            pltpu.VMEM((block, width), BF16),
            pltpu.VMEM((taken, depth), BF16),
            pltpu.VMEM((total, 2 * FOLD * hid), BF16),
            pltpu.VMEM((total, total), BF16),
            pltpu.VMEM((total, taken), BF16),
            pltpu.VMEM((block, width), F32),
            pltpu.VMEM((block, block), BF16),
            pltpu.VMEM((block, width), F32),
            pltpu.VMEM((block, 128), F32),
            dma((3,)), dma((3,)), dma((3,)),
            dma((peers,)), dma((peers,)), dma((peers,)), dma((peers,)),
            dma((2,)), dma((2,)),
            pltpu.SemaphoreType.REGULAR,
        ],
        compiler_params=pltpu.CompilerParams(
            collective_id=0, has_side_effects=True, vmem_limit_bytes=48 * 2**20
        ),
        name="relay",
    )(acts, norm_gain, router, w_gate, w_up, w_down, expert_ids)


def solution(mesh):
    sections, et = mesh.shape["section"], mesh.shape["et"]
    side = math.isqrt(et // 2)
    return jax.shard_map(
        functools.partial(body, sections, side),
        mesh=mesh,
        in_specs=(
            P("section", "et", None),
            P("section", None),
            P("section", None, None),
            P("section", None, "et"),
            P("section", None, "et"),
            P("section", "et", None),
            P("section", None, "et", None),
        ),
        out_specs=P("section", "et", None),
        check_vma=False,
    )
```

time: 1510 us -> 245 us (0.16)
  waiting for transfers between devices: 1350 us -> 0 us
  Pallas kernels: 0 us -> 236 us
  matrix products: 85.8 us -> 0 us
  local copies, waits for them, and re-layouts: 38.7 us -> 6.61 us
    unnamed x24 -> x0, waiting for transfers between devices: 927 us -> none
    all_gather x8 -> x0, waiting for transfers between devices: 384 us -> none  [expert_layer(): piece = lax.all_gather(slots, 'et', axis=0, tiled=True)]
    pallas_call x0 -> x1, Pallas kernels: none -> 236 us  [body(): pl.pallas_call(functools.partial(relay_kernel, sections, side), out_shape...]
    dot_general x40 -> x0, matrix products: 85.8 us -> none  [the longest x8 43 us: expert_layer(): jnp.dot(hidden, w_down, preferred_element_type=jnp.float32)]
    ppermute x8 -> x0, waiting for transfers between devices: 43.2 us -> none  [shifted(): lax.ppermute(x, axis, [(i, (i + by) % devices) for i in range(devices)])]
    unnamed x32 -> x9, local copies, waits for them, and re-layouts: 37.1 us -> 6.61 us
  transfers between devices with their start and end apart: 24 -> 0, of which waited for: 24 -> 0; matrix products, arithmetic and copies ran while one was open for 0% -> 0% of each run, Pallas kernels for 0% -> 0%
where the time goes in v1:
time: 245 us; the launch traced here: 243 us
  Pallas kernels  236 us (96%)
  local copies, waits for them, and re-layouts  6.61 us (3%)
    pallas_call x1, Pallas kernels, body(): pl.pallas_call(functools.partial(relay_kernel, sections, side), out_shape...  236 us
    unnamed x9, local copies, waits for them, and re-layouts  6.61 us

profile of v1, /device:TPU:6, one launch (start us, length us, event | category | flops | bytes accessed | tf_op | source)
XLA Modules:
  0.0 243.0 jit_solution(17403179591179128135)
XLA Ops:
  0.0 0.8 copy.9.ids
  0.8 1.6 copy.8.router
  2.4 0.0 copy-start
  2.4 1.9 copy-done
  4.3 0.0 copy-start.1
  4.3 0.9 copy-done.1
  5.2 0.0 copy-start.2
  5.2 0.7 copy-done.2
  5.9 236.4 %relay.1 = bf16[1,16,6144]{2,1,0:T(8,128)(2,1)S(1)} custom-call(bf16[1,16,6144]{2,1,0:T(8,128)(2,1)S(1)} %copy-done.1, f32[1,6144]{1,0:T(1,128)S(1)} %copy-done.2, bf16[1,6144,8]{2,1,0:T(8,128)(2,1)S(1)} %copy.8.router, bf16[1,6144,256]{2,1,0:T(8,128)(2,1)S(1)} %copy-done, bf16[1,6144,256]{2,1,0:T(8,128)(2,1)} %w_up.1, bf16[1,256,6144]{2,1,0:T(8,128)(2,1)} %w_down.1, ...), custom_call_target="tpu_custom_call" | custom-call | tf_op jit(solution)/shard_map/relay/pallas_call | solution.py:294
  242.3 0.7 copy.11
Async XLA Ops:
  2.4 1.9 copy-start
  4.3 0.9 copy-start.1
  5.2 0.7 copy-start.2

commit v2 on v1

v2 whole, which is shorter than its diff:
```python
import functools
import math

import jax
import jax.numpy as jnp
from jax import lax
from jax.experimental import pallas as pl
from jax.experimental.pallas import tpu as pltpu
from jax.sharding import PartitionSpec as P

MESH = pl.DeviceIdType.MESH
F32 = jnp.float32
BF16 = jnp.bfloat16
CAP = 4
FOLD = 4
PATHS = 2
EPS = 1e-05


def iota(shape, dim):
    return lax.broadcasted_iota(jnp.int32, shape, dim)


def contract(a, b, dim_a, dim_b):
    return lax.dot_general(a, b, (((dim_a,), (dim_b,)), ((), ())), preferred_element_type=F32)


def far_first(side):
    return sorted(range(1, side), key=lambda d: (-min(d, side - d), d))


def relay_kernel(
    sections, side, acts_hbm, gain_hbm, router_hbm, w_gate, w_up, w_down, ids_hbm, out,
    acts, gain, router, ids,
    wg, wu, wd, gathered, terms, mid, mid_sum, landed, rows, chosen, early_out, early_in, late_out, late_in,
    xg, sums_gu, spread, perm, grow, gain_fold, next_route, next_pre, gates,
    in_sem, w_local, w_send, w_recv, ag1_send, ag1_recv, ag2_send, ag2_recv,
    rs1_send, rs1_recv, rs2_send, rs2_recv, z_send, z_recv, credit,
):
    chips = side * side
    n_rows, depth = acts.shape[1], acts.shape[2]
    part = depth // PATHS
    width = part // FOLD
    hid = w_down.shape[1]
    lanes = FOLD * n_rows
    block = FOLD * CAP
    total = chips * block
    taken = chips * CAP

    section = lax.axis_index("section")
    et = lax.axis_index("et")
    core = lax.rem(et, 2)
    chip = et // 2
    cx = chip // side
    cy = lax.rem(chip, side)

    def chip_at(dx, dy):
        return lax.rem(cx + dx, side) * side + lax.rem(cy + dy, side)

    def device_at(dx, dy):
        return (section, chip_at(dx, dy) * 2 + core)

    def along(axis, d):
        return (d, 0) if axis == 0 else (0, d)

    def place(axis):
        return cx if axis == 0 else cy

    order = far_first(side)
    sibling = (section, chip * 2 + 1 - core)
    above = (lax.rem(section + 1, sections), et)
    below = (lax.rem(section + sections - 1, sections), et)

    barrier = pltpu.get_barrier_semaphore()
    partners = [device_at(*along(axis, d)) for axis in range(2) for d in order] + [sibling, above, below]
    for device in partners:
        pl.semaphore_signal(barrier, inc=1, device_id=device, device_id_type=MESH)

    inputs = [
        pltpu.make_async_copy(src, dst, in_sem.at[i])
        for i, (src, dst) in enumerate(
            ((acts_hbm, acts), (ids_hbm, ids), (gain_hbm, gain), (router_hbm, router))
        )
    ]
    for copy in inputs:
        copy.start()
    pieces = []
    for p in range(PATHS):
        for src, dst in ((w_gate, wg), (w_up, wu)):
            span = pl.ds(p * part, part)
            pieces.append((src.at[0, span], dst.at[0, span], dst.at[1, span]))
    pieces.append((w_down.at[0], wd.at[0], wd.at[1]))
    loads = [pltpu.make_async_copy(src, dst, w_local.at[i]) for i, (src, dst, _) in enumerate(pieces)]
    for load in loads:
        load.start()

    def routing(turn):
        batch = lax.rem(section - turn + 2 * sections, sections)
        both = ids[0, batch].astype(F32).astype(BF16)
        tile = jnp.where(iota((n_rows, lanes), 0) == lax.rem(iota((n_rows, lanes), 1), n_rows), 1.0, 0.0)
        lane_ids = jnp.dot(both, tile.astype(BF16), preferred_element_type=F32)
        first, second = lane_ids[0:1, :], lane_ids[1:2, :]
        held = jnp.where((first == 0.0) | (second == 0.0), 1.0, 0.0) * (turn <= section).astype(F32)
        other = (first + second) * held
        i = iota((lanes, lanes), 0)
        j = iota((lanes, lanes), 1)
        upto = jnp.where((i // n_rows == j // n_rows) & (i <= j), 1.0, 0.0).astype(BF16)
        spots = jnp.dot(jnp.broadcast_to(held, (8, lanes)).astype(BF16), upto, preferred_element_type=F32)
        spot = spots[0:1, :] - 1.0
        keep = jnp.where((i == j) & (held == 0.0), 1.0, 0.0).astype(BF16)
        i = iota((block, lanes), 0)
        j = iota((block, lanes), 1)
        match = (i // CAP == j // n_rows) & (lax.rem(i, CAP).astype(F32) == spot) & (held > 0.0)
        select = jnp.where(match, 1.0, 0.0)
        rival = jnp.sum(select * other, axis=1, keepdims=True)
        valid = jnp.sum(select, axis=1, keepdims=True)
        return select.astype(BF16), rival, valid, keep

    i = iota((total, total), 0)
    j = iota((total, total), 1)
    source = lax.rem(i, taken) // CAP * block + i // taken * CAP + lax.rem(i, CAP)
    perm[...] = jnp.where(j == source, 1.0, 0.0).astype(BF16)
    i = iota((total, taken), 0)
    j = iota((total, taken), 1)
    grow[...] = jnp.where(j == i // block * CAP + lax.rem(i, CAP), 1.0, 0.0).astype(BF16)
    fold_of = iota((block, 1), 0) // CAP

    def columns(p, a):
        return slice(p * part + a * width, p * part + (a + 1) * width)

    inputs[0].wait()
    inputs[1].wait()
    select, _, _, _ = routing(0)
    for p in range(PATHS):
        for a in range(FOLD):
            rows[p, a * n_rows : (a + 1) * n_rows, :] = acts[0, :, columns(p, a)]
        chosen[p] = jnp.dot(select, rows[p], preferred_element_type=F32).astype(BF16)

    pl.semaphore_wait(barrier, len(partners))

    def remote(src, dst, send, recv, device):
        return pltpu.make_async_remote_copy(
            src_ref=src, dst_ref=dst, send_sem=send, recv_sem=recv, device_id=device, device_id_type=MESH
        )

    def own_chip(p, d):
        dx, dy = along(p, side - d)
        return chip_at(dx, dy) if d else chip

    gather1 = [
        {
            d: remote(
                chosen.at[p], gathered.at[p, chip], ag1_send.at[p, d - 1], ag1_recv.at[p, d - 1],
                device_at(*along(p, d)),
            )
            for d in order
        }
        for p in range(PATHS)
    ]
    gather2 = [
        {
            (d, e): remote(
                chosen.at[p] if d == 0 else gathered.at[p, own_chip(p, d)],
                gathered.at[p, own_chip(p, d)],
                ag2_send.at[p, d, e - 1], ag2_recv.at[p, d, e - 1],
                device_at(*along(1 - p, e)),
            )
            for d in range(side)
            for e in order
        }
        for p in range(PATHS)
    ]
    scatter1 = [
        {
            (d, e): remote(
                terms.at[p, chip_at(*(d, e) if p == 0 else (e, d))],
                mid.at[p, side - e, d],
                rs1_send.at[p, d, e - 1], rs1_recv.at[p, d, e - 1],
                device_at(*along(1 - p, e)),
            )
            for d in range(side)
            for e in order
        }
        for p in range(PATHS)
    ]
    scatter2 = [
        {
            d: remote(
                mid_sum.at[p, d], landed.at[p, side - d], rs2_send.at[p, d - 1], rs2_recv.at[p, d - 1],
                device_at(*along(p, d)),
            )
            for d in order
        }
        for p in range(PATHS)
    ]
    early = remote(early_out, early_in, z_send.at[PATHS], z_recv.at[PATHS], above)
    late = [remote(late_out.at[p], late_in.at[p], z_send.at[p], z_recv.at[p], above) for p in range(PATHS)]
    swaps = [remote(src, dst, w_send.at[i], w_recv.at[i], sibling) for i, (src, _, dst) in enumerate(pieces)]

    def start_gather(p):
        for d in order:
            gather1[p][d].start()
        for e in order:
            gather2[p][0, e].start()
        gathered[p, chip] = chosen[p]

    def merged(p):
        incoming = contract(early_in[PATHS * lanes :, 0:lanes], late_in[p], 0, 0)
        return (early_in[p * lanes : (p + 1) * lanes, :].astype(F32) + incoming).astype(BF16)

    for p in range(PATHS):
        start_gather(p)
    for swap in swaps:
        swap.start()

    inputs[2].wait()
    inputs[3].wait()
    for p in range(PATHS):
        folded = jnp.zeros((block, width), F32)
        for a in range(FOLD):
            folded = jnp.where(fold_of == a, gain[0:1, columns(p, a)], folded)
        gain_fold[p] = folded

    def turn_body(turn, carry):
        for d in reversed(order):
            for p in range(PATHS):
                gather1[p][d].wait_recv()
                for e in order:
                    gather2[p][d, e].start()

        @pl.when(turn > 0)
        def _():
            for p in range(PATHS):
                rows[p] = merged(p)
            pl.semaphore_signal(credit, inc=1, device_id=below, device_id_type=MESH)

        select, rival, valid, keep = routing(turn)

        @pl.when(turn > 0)
        def _():
            early.wait_send()

        for p in range(PATHS):
            early_out[p * lanes : (p + 1) * lanes, :] = jnp.dot(
                keep, rows[p], preferred_element_type=F32
            ).astype(BF16)
        early_out[PATHS * lanes :, 0:lanes] = select

        @pl.when(turn > 0)
        def _():
            pl.semaphore_wait(credit, 1)

        early.start()

        partial = jnp.zeros((block, router.shape[1]), F32)
        square = jnp.zeros((block, 1), F32)
        for p in range(PATHS):
            x = chosen[p].astype(F32)
            weighted = (x * gain_fold[p]).astype(BF16)
            square = square + jnp.sum(x * x, axis=1, keepdims=True)
            for a in range(FOLD):
                piece = contract(weighted, router[0, :, columns(p, a)], 1, 1)
                partial = partial + jnp.where(fold_of == a, piece, 0.0)
        logits = jnp.zeros_like(partial)
        squares = jnp.zeros_like(square)
        row_slot = lax.rem(iota((block, 1), 0), CAP)
        for slot in range(CAP):
            here = row_slot == slot
            logits = jnp.where(here, jnp.sum(jnp.where(here, partial, 0.0), axis=0, keepdims=True), logits)
            squares = jnp.where(here, jnp.sum(jnp.where(here, square, 0.0), axis=0, keepdims=True), squares)
        logits = logits * lax.rsqrt(squares / depth + EPS)
        expert = iota(logits.shape, 1).astype(F32)
        l_rival = jnp.sum(jnp.where(expert == rival, logits, 0.0), axis=1, keepdims=True)
        gates[...] = jnp.broadcast_to(valid * jax.nn.sigmoid(logits[:, 0:1] - l_rival), gates.shape)

        square = jnp.zeros((taken, 1), F32)
        for p in range(PATHS):
            for d in (0, *reversed(order)):
                for e in reversed(order):
                    gather2[p][d, e].wait_recv()
            everyone = gathered[p].reshape(total, width)
            ordered = jnp.dot(perm[...], everyone, preferred_element_type=F32)
            for a in range(FOLD):
                piece = ordered[a * taken : (a + 1) * taken, :]
                square = square + jnp.sum(piece * piece, axis=1, keepdims=True)
                xg[:, a * width : (a + 1) * width] = (piece * gain[0:1, columns(p, a)]).astype(BF16)

            @pl.when(turn == 0)
            def _():
                for n in (2 * p, 2 * p + 1):
                    loads[n].wait()
                    swaps[n].wait()

            for half in range(2):
                for n, w in ((0, wg), (1, wu)):
                    dot = jnp.dot(xg[...], w[half, p * part : (p + 1) * part, :], preferred_element_type=F32)
                    span = slice((2 * n + half) * hid, (2 * n + half + 1) * hid)
                    if p == 0:
                        sums_gu[:, span] = dot
                    else:
                        sums_gu[:, span] = sums_gu[:, span] + dot
        scale = lax.rsqrt(square / depth + EPS)
        row_fold = lax.rem(iota((total, hid), 0), block) // CAP
        for half in range(2):
            g = sums_gu[:, half * hid : (half + 1) * hid] * scale
            u = sums_gu[:, (2 + half) * hid : (3 + half) * hid] * scale
            wide = jnp.dot(grow[...], (jax.nn.silu(g) * u).astype(BF16), preferred_element_type=F32)
            for a in range(FOLD):
                spread[:, (a * 2 + half) * hid : (a * 2 + half + 1) * hid] = jnp.where(
                    row_fold == a, wide, 0.0
                ).astype(BF16)

        @pl.when(turn == 0)
        def _():
            loads[4].wait()
            swaps[4].wait()

        step = math.gcd(width, 256)
        for p in range(PATHS):
            for n in range(0, width, step):
                acc = jnp.zeros((total, step), F32)
                for a in range(FOLD):
                    begin = p * part + a * width + n
                    for half in range(2):
                        acc = acc + jnp.dot(
                            spread[:, (a * 2 + half) * hid : (a * 2 + half + 1) * hid],
                            wd[half, :, begin : begin + step],
                            preferred_element_type=F32,
                        )
                terms[p, :, :, n : n + step] = acc.astype(BF16).reshape(chips, block, step)
            if p == PATHS - 1:
                for q in range(PATHS):
                    for copy in (*gather1[q].values(), *gather2[q].values()):
                        copy.wait_send()
            for d in (*order, 0):
                for e in order:
                    scatter1[p][d, e].start()

        for d in (*order, 0):
            for p in range(PATHS):
                here = chip_at(*along(p, d))
                value = terms[p, here].astype(F32)
                for e in reversed(order):
                    scatter1[p][d, e].wait_recv()
                    value = value + mid[p, side - e, d].astype(F32)
                if d:
                    mid_sum[p, d] = value.astype(BF16)
                    scatter2[p][d].start()
                else:
                    landed[p, 0] = value.astype(BF16)

        early.wait_recv()
        ahead, _, _, _ = routing(turn + 1)
        next_route[...] = contract(ahead, early_in[PATHS * lanes :, 0:lanes], 1, 1).astype(BF16)
        for p in range(PATHS):
            next_pre[p] = jnp.dot(ahead, early_in[p * lanes : (p + 1) * lanes, :], preferred_element_type=F32)

        for p in range(PATHS):

            @pl.when(turn > 0)
            def _():
                late[p].wait_send()

            result = landed[p, 0].astype(F32)
            for d in reversed(order):
                scatter2[p][d].wait_recv()
                result = result + landed[p, side - d].astype(F32)
            late_out[p] = (chosen[p].astype(F32) + gates[:, 0:1] * result).astype(BF16)
            late[p].start()
        for p in range(PATHS):
            for copy in (*scatter1[p].values(), *scatter2[p].values()):
                copy.wait_send()
        for p in range(PATHS):
            late[p].wait_recv()
            picked = next_pre[p] + jnp.dot(next_route[...], late_in[p], preferred_element_type=F32)

            @pl.when(turn < sections - 1)
            def _():
                chosen[p] = picked.astype(BF16)
                start_gather(p)

        return carry

    lax.fori_loop(0, sections, turn_body, 0)

    for p in range(PATHS):
        final = merged(p)
        for a in range(FOLD):
            out[0, :, columns(p, a)] = final[a * n_rows : (a + 1) * n_rows, :]
    early.wait_send()
    for p in range(PATHS):
        late[p].wait_send()


def body(sections, side, acts, norm_gain, router, w_gate, w_up, w_down, expert_ids):
    chips = side * side
    n_rows, depth = acts.shape[1], acts.shape[2]
    part = depth // PATHS
    width = part // FOLD
    hid = w_gate.shape[2]
    lanes = FOLD * n_rows
    block = FOLD * CAP
    total = chips * block
    taken = chips * CAP
    router = jnp.transpose(router, (0, 2, 1))
    expert_ids = jnp.transpose(expert_ids, (0, 1, 3, 2))
    hbm = pl.BlockSpec(memory_space=pl.ANY)
    dma = pltpu.SemaphoreType.DMA
    return pl.pallas_call(
        functools.partial(relay_kernel, sections, side),
        out_shape=jax.ShapeDtypeStruct(acts.shape, acts.dtype),
        in_specs=[hbm] * 7,
        out_specs=pl.BlockSpec(memory_space=pltpu.VMEM),
        scratch_shapes=[
            pltpu.VMEM(acts.shape, BF16),
            pltpu.VMEM(norm_gain.shape, F32),
            pltpu.VMEM(router.shape, BF16),
            pltpu.VMEM(expert_ids.shape, jnp.int32),
            pltpu.VMEM((2, depth, hid), BF16),
            pltpu.VMEM((2, depth, hid), BF16),
            pltpu.VMEM((2, hid, depth), BF16),
            pltpu.VMEM((PATHS, chips, block, width), BF16),
            pltpu.VMEM((PATHS, chips, block, width), BF16),
            pltpu.VMEM((PATHS, side, side, block, width), BF16),
            pltpu.VMEM((PATHS, side, block, width), BF16),
            pltpu.VMEM((PATHS, side, block, width), BF16),
            pltpu.VMEM((PATHS, lanes, width), BF16),
            pltpu.VMEM((PATHS, block, width), BF16),
            pltpu.VMEM((PATHS * lanes + block, width), BF16),
            pltpu.VMEM((PATHS * lanes + block, width), BF16),
            pltpu.VMEM((PATHS, block, width), BF16),
            pltpu.VMEM((PATHS, block, width), BF16),
            pltpu.VMEM((taken, part), BF16),
            pltpu.VMEM((taken, 4 * hid), F32),
            pltpu.VMEM((total, 2 * FOLD * hid), BF16),
            pltpu.VMEM((total, total), BF16),
            pltpu.VMEM((total, taken), BF16),
            pltpu.VMEM((PATHS, block, width), F32),
            pltpu.VMEM((block, block), BF16),
            pltpu.VMEM((PATHS, block, width), F32),
            pltpu.VMEM((block, 128), F32),
            dma((4,)), dma((5,)), dma((5,)), dma((5,)),
            dma((PATHS, side - 1)), dma((PATHS, side - 1)),
            dma((PATHS, side, side - 1)), dma((PATHS, side, side - 1)),
            dma((PATHS, side, side - 1)), dma((PATHS, side, side - 1)),
            dma((PATHS, side - 1)), dma((PATHS, side - 1)),
            dma((PATHS + 1,)), dma((PATHS + 1,)),
            pltpu.SemaphoreType.REGULAR,
        ],
        compiler_params=pltpu.CompilerParams(
            collective_id=0, has_side_effects=True, vmem_limit_bytes=60 * 2**20
        ),
        name="relay",
    )(acts, norm_gain, router, w_gate, w_up, w_down, expert_ids)


def solution(mesh):
    sections, et = mesh.shape["section"], mesh.shape["et"]
    side = math.isqrt(et // 2)
    return jax.shard_map(
        functools.partial(body, sections, side),
        mesh=mesh,
        in_specs=(
            P("section", "et", None),
            P("section", None),
            P("section", None, None),
            P("section", None, "et"),
            P("section", None, "et"),
            P("section", "et", None),
            P("section", None, "et", None),
        ),
        out_specs=P("section", "et", None),
        check_vma=False,
    )
```

time: 245 us -> 223 us (0.910)
  Pallas kernels: 236 us -> 221 us
  local copies, waits for them, and re-layouts: 6.61 us -> 1.62 us
    pallas_call x1, Pallas kernels: 236 us -> 221 us  [body(): pl.pallas_call(functools.partial(relay_kernel, sections, side), out_shape...]
    unnamed x9 -> x1, local copies, waits for them, and re-layouts: 6.61 us -> 1.62 us
where the time goes in v2:
time: 223 us; the launch traced here: 222 us
  Pallas kernels  221 us (99%)
    pallas_call x1, Pallas kernels, body(): pl.pallas_call(functools.partial(relay_kernel, sections, side), out_shape...  221 us

profile of v2, /device:TPU:6, one launch (start us, length us, event | category | flops | bytes accessed | tf_op | source)
XLA Modules:
  0.0 222.4 jit_solution(12867497092637992072)
XLA Ops:
  0.0 220.8 %relay.1 = bf16[1,16,6144]{2,1,0:T(8,128)(2,1)} custom-call(bf16[1,16,6144]{2,1,0:T(8,128)(2,1)} %acts_hbm.1, f32[1,6144]{1,0:T(1,128)} %gain_hbm.1, bf16[1,8,6144]{2,1,0:T(8,128)(2,1)} %bitcast.2, bf16[1,6144,256]{2,1,0:T(8,128)(2,1)} %w_gate.1, bf16[1,6144,256]{2,1,0:T(8,128)(2,1)} %w_up.1, bf16[1,256,6144]{2,1,0:T(8,128)(2,1)} %w_down.1, ...), custom_call_target="tpu_custom_call" | custom-call | tf_op jit(solution)/shard_map/relay/pallas_call | solution.py:409
  220.8 1.6 copy.9

commit v3 on v2

--- a/solution.py
+++ b/solution.py
@@ -32,10 +32,10 @@
 def relay_kernel(
     sections, side, acts_hbm, gain_hbm, router_hbm, w_gate, w_up, w_down, ids_hbm, out,
     acts, gain, router, ids,
-    wg, wu, wd, gathered, terms, mid, mid_sum, landed, rows, chosen, early_out, early_in, late_out, late_in,
-    xg, sums_gu, spread, perm, grow, gain_fold, next_route, next_pre, gates,
-    in_sem, w_local, w_send, w_recv, ag1_send, ag1_recv, ag2_send, ag2_recv,
-    rs1_send, rs1_recv, rs2_send, rs2_recv, z_send, z_recv, credit,
+    wg, wu, wd, gathered, terms, mid, mid_sum, landed, rows, chosen, early_out, early_in, fresh,
+    xg, sums_gu, hidden, stacked, perm, perm_back, gain_fold, next_route, next_pre, gates_out, gates_in,
+    in_sem, w_local, w_send, w_recv, ag_send, ag1_recv, ag2_recv,
+    rs1_send, rs1_recv, rs2_send, rs2_recv, z_send, z_recv, credit_early, credit_landed,
 ):
     chips = side * side
     n_rows, depth = acts.shape[1], acts.shape[2]
@@ -68,18 +68,26 @@
 
     order = far_first(side)
     sibling = (section, chip * 2 + 1 - core)
-    above = (lax.rem(section + 1, sections), et)
-    below = (lax.rem(section + sections - 1, sections), et)
+    next_section = lax.rem(section + 1, sections)
+    last_section = lax.rem(section + sections - 1, sections)
+    above = (next_section, chip * 2 + 1 - core)
+    below = (last_section, chip * 2 + 1 - core)
 
     barrier = pltpu.get_barrier_semaphore()
-    partners = [device_at(*along(axis, d)) for axis in range(2) for d in order] + [sibling, above, below]
+    partners = [sibling, above, below]
+    for axis in range(2):
+        for d in order:
+            there = chip_at(*along(axis, d)) * 2
+            partners += [
+                (section, there + core), (next_section, there + 1 - core), (last_section, there + 1 - core)
+            ]
     for device in partners:
         pl.semaphore_signal(barrier, inc=1, device_id=device, device_id_type=MESH)
 
     inputs = [
         pltpu.make_async_copy(src, dst, in_sem.at[i])
         for i, (src, dst) in enumerate(
-            ((acts_hbm, acts), (ids_hbm, ids), (gain_hbm, gain), (router_hbm, router))
+            ((acts_hbm, acts), (ids_hbm.at[0], ids.at[0]), (gain_hbm, gain), (router_hbm, router))
         )
     ]
     for copy in inputs:
@@ -89,14 +97,14 @@
         for src, dst in ((w_gate, wg), (w_up, wu)):
             span = pl.ds(p * part, part)
             pieces.append((src.at[0, span], dst.at[0, span], dst.at[1, span]))
-    pieces.append((w_down.at[0], wd.at[0], wd.at[1]))
+    pieces.append((w_down.at[0], wd.at[pl.ds(0, hid)], wd.at[pl.ds(hid, hid)]))
     loads = [pltpu.make_async_copy(src, dst, w_local.at[i]) for i, (src, dst, _) in enumerate(pieces)]
     for load in loads:
         load.start()
 
     def routing(turn):
         batch = lax.rem(section - turn + 2 * sections, sections)
-        both = ids[0, batch].astype(F32).astype(BF16)
+        both = ids[lax.rem(turn, 2), batch].astype(F32).astype(BF16)
         tile = jnp.where(iota((n_rows, lanes), 0) == lax.rem(iota((n_rows, lanes), 1), n_rows), 1.0, 0.0)
         lane_ids = jnp.dot(both, tile.astype(BF16), preferred_element_type=F32)
         first, second = lane_ids[0:1, :], lane_ids[1:2, :]
@@ -120,9 +128,8 @@
     j = iota((total, total), 1)
     source = lax.rem(i, taken) // CAP * block + i // taken * CAP + lax.rem(i, CAP)
     perm[...] = jnp.where(j == source, 1.0, 0.0).astype(BF16)
-    i = iota((total, taken), 0)
-    j = iota((total, taken), 1)
-    grow[...] = jnp.where(j == i // block * CAP + lax.rem(i, CAP), 1.0, 0.0).astype(BF16)
+    source = lax.rem(i, block) // CAP * taken + i // block * CAP + lax.rem(i, CAP)
+    perm_back[...] = jnp.where(j == source, 1.0, 0.0).astype(BF16)
     fold_of = iota((block, 1), 0) // CAP
 
     def columns(p, a):
@@ -150,7 +157,7 @@
     gather1 = [
         {
             d: remote(
-                chosen.at[p], gathered.at[p, chip], ag1_send.at[p, d - 1], ag1_recv.at[p, d - 1],
+                chosen.at[p], gathered.at[p, chip], ag_send.at[p], ag1_recv.at[p, d - 1],
                 device_at(*along(p, d)),
             )
             for d in order
@@ -162,7 +169,7 @@
             (d, e): remote(
                 chosen.at[p] if d == 0 else gathered.at[p, own_chip(p, d)],
                 gathered.at[p, own_chip(p, d)],
-                ag2_send.at[p, d, e - 1], ag2_recv.at[p, d, e - 1],
+                ag_send.at[p], ag2_recv.at[p],
                 device_at(*along(1 - p, e)),
             )
             for d in range(side)
@@ -175,7 +182,7 @@
             (d, e): remote(
                 terms.at[p, chip_at(*(d, e) if p == 0 else (e, d))],
                 mid.at[p, side - e, d],
-                rs1_send.at[p, d, e - 1], rs1_recv.at[p, d, e - 1],
+                rs1_send.at[p], rs1_recv.at[p, d],
                 device_at(*along(1 - p, e)),
             )
             for d in range(side)
@@ -186,15 +193,26 @@
     scatter2 = [
         {
             d: remote(
-                mid_sum.at[p, d], landed.at[p, side - d], rs2_send.at[p, d - 1], rs2_recv.at[p, d - 1],
-                device_at(*along(p, d)),
+                mid_sum.at[p, d], landed.at[p, (side - d) % side], rs2_send.at[p], rs2_recv.at[p],
+                (next_section, chip_at(*along(p, d)) * 2 + 1 - core),
             )
-            for d in order
+            for d in range(side)
         }
         for p in range(PATHS)
     ]
-    early = remote(early_out, early_in, z_send.at[PATHS], z_recv.at[PATHS], above)
-    late = [remote(late_out.at[p], late_in.at[p], z_send.at[p], z_recv.at[p], above) for p in range(PATHS)]
+    early = [
+        remote(early_out, early_in, z_send.at[0], z_recv.at[0], above),
+        remote(gates_out, gates_in, z_send.at[1], z_recv.at[1], above),
+    ]
+    swap_ids = remote(ids.at[0], ids.at[1], w_send.at[len(pieces)], w_recv.at[len(pieces)], sibling)
+    few, many = side - 1, side * (side - 1)
+
+    def sent(ref, sem):
+        remote(ref, ref, sem, sem, sibling).wait_send()
+
+    def came(ref, sem):
+        remote(ref, ref, sem, sem, sibling).wait_recv()
+
     swaps = [remote(src, dst, w_send.at[i], w_recv.at[i], sibling) for i, (src, _, dst) in enumerate(pieces)]
 
     def start_gather(p):
@@ -204,12 +222,16 @@
             gather2[p][0, e].start()
         gathered[p, chip] = chosen[p]
 
+    routes = slice(PATHS * lanes, PATHS * lanes + block)
+    slots_at = [slice(routes.stop + p * block, routes.stop + (p + 1) * block) for p in range(PATHS)]
+
     def merged(p):
-        incoming = contract(early_in[PATHS * lanes :, 0:lanes], late_in[p], 0, 0)
+        incoming = contract(early_in[routes, 0:lanes], fresh[p], 0, 0)
         return (early_in[p * lanes : (p + 1) * lanes, :].astype(F32) + incoming).astype(BF16)
 
     for p in range(PATHS):
         start_gather(p)
+    swap_ids.start()
     for swap in swaps:
         swap.start()
 
@@ -222,8 +244,14 @@
         gain_fold[p] = folded
 
     def turn_body(turn, carry):
-        for d in reversed(order):
-            for p in range(PATHS):
+        for p in range(PATHS):
+            if p == PATHS - 1:
+
+                @pl.when(turn > 0)
+                def _():
+                    pl.semaphore_wait(credit_landed, 1)
+
+            for d in reversed(order):
                 gather1[p][d].wait_recv()
                 for e in order:
                     gather2[p][d, e].start()
@@ -232,25 +260,9 @@
         def _():
             for p in range(PATHS):
                 rows[p] = merged(p)
-            pl.semaphore_signal(credit, inc=1, device_id=below, device_id_type=MESH)
+            pl.semaphore_signal(credit_early, inc=1, device_id=below, device_id_type=MESH)
 
         select, rival, valid, keep = routing(turn)
-
-        @pl.when(turn > 0)
-        def _():
-            early.wait_send()
-
-        for p in range(PATHS):
-            early_out[p * lanes : (p + 1) * lanes, :] = jnp.dot(
-                keep, rows[p], preferred_element_type=F32
-            ).astype(BF16)
-        early_out[PATHS * lanes :, 0:lanes] = select
-
-        @pl.when(turn > 0)
-        def _():
-            pl.semaphore_wait(credit, 1)
-
-        early.start()
 
         partial = jnp.zeros((block, router.shape[1]), F32)
         square = jnp.zeros((block, 1), F32)
@@ -271,13 +283,31 @@
         logits = logits * lax.rsqrt(squares / depth + EPS)
         expert = iota(logits.shape, 1).astype(F32)
         l_rival = jnp.sum(jnp.where(expert == rival, logits, 0.0), axis=1, keepdims=True)
-        gates[...] = jnp.broadcast_to(valid * jax.nn.sigmoid(logits[:, 0:1] - l_rival), gates.shape)
+        gate = valid * jax.nn.sigmoid(logits[:, 0:1] - l_rival)
+
+        @pl.when(turn > 0)
+        def _():
+            for copy in early:
+                copy.wait_send()
+
+        for p in range(PATHS):
+            early_out[p * lanes : (p + 1) * lanes, :] = jnp.dot(
+                keep, rows[p], preferred_element_type=F32
+            ).astype(BF16)
+            early_out[slots_at[p], :] = chosen[p]
+        early_out[routes, 0:lanes] = select
+        gates_out[...] = jnp.broadcast_to(gate, gates_out.shape)
+
+        @pl.when(turn > 0)
+        def _():
+            pl.semaphore_wait(credit_early, 1)
+
+        for copy in early:
+            copy.start()
 
         square = jnp.zeros((taken, 1), F32)
         for p in range(PATHS):
-            for d in (0, *reversed(order)):
-                for e in reversed(order):
-                    gather2[p][d, e].wait_recv()
+            came(gathered.at[p, pl.ds(0, many)], ag2_recv.at[p])
             everyone = gathered[p].reshape(total, width)
             ordered = jnp.dot(perm[...], everyone, preferred_element_type=F32)
             for a in range(FOLD):
@@ -300,85 +330,75 @@
                     else:
                         sums_gu[:, span] = sums_gu[:, span] + dot
         scale = lax.rsqrt(square / depth + EPS)
-        row_fold = lax.rem(iota((total, hid), 0), block) // CAP
         for half in range(2):
             g = sums_gu[:, half * hid : (half + 1) * hid] * scale
             u = sums_gu[:, (2 + half) * hid : (3 + half) * hid] * scale
-            wide = jnp.dot(grow[...], (jax.nn.silu(g) * u).astype(BF16), preferred_element_type=F32)
-            for a in range(FOLD):
-                spread[:, (a * 2 + half) * hid : (a * 2 + half + 1) * hid] = jnp.where(
-                    row_fold == a, wide, 0.0
-                ).astype(BF16)
+            hidden[:, half * hid : (half + 1) * hid] = (jax.nn.silu(g) * u).astype(BF16)
 
         @pl.when(turn == 0)
         def _():
             loads[4].wait()
             swaps[4].wait()
 
-        step = math.gcd(width, 256)
-        for p in range(PATHS):
-            for n in range(0, width, step):
-                acc = jnp.zeros((total, step), F32)
-                for a in range(FOLD):
-                    begin = p * part + a * width + n
-                    for half in range(2):
-                        acc = acc + jnp.dot(
-                            spread[:, (a * 2 + half) * hid : (a * 2 + half + 1) * hid],
-                            wd[half, :, begin : begin + step],
-                            preferred_element_type=F32,
-                        )
-                terms[p, :, :, n : n + step] = acc.astype(BF16).reshape(chips, block, step)
-            if p == PATHS - 1:
+        for p in range(PATHS):
+            for a in range(FOLD):
+                stacked[a * taken : (a + 1) * taken, :] = jnp.dot(
+                    hidden[...], wd[:, columns(p, a)], preferred_element_type=F32
+                ).astype(BF16)
+            reordered = jnp.dot(perm_back[...], stacked[...], preferred_element_type=F32)
+            terms[p] = reordered.astype(BF16).reshape(chips, block, width)
+            if p == 0:
                 for q in range(PATHS):
-                    for copy in (*gather1[q].values(), *gather2[q].values()):
-                        copy.wait_send()
+                    sent(gathered.at[q, pl.ds(0, few + many)], ag_send.at[q])
             for d in (*order, 0):
                 for e in order:
                     scatter1[p][d, e].start()
 
-        for d in (*order, 0):
-            for p in range(PATHS):
+        for p in range(PATHS):
+            for d in (*order, 0):
                 here = chip_at(*along(p, d))
                 value = terms[p, here].astype(F32)
+                came(mid.at[p, 0, pl.ds(0, few)], rs1_recv.at[p, d])
                 for e in reversed(order):
-                    scatter1[p][d, e].wait_recv()
                     value = value + mid[p, side - e, d].astype(F32)
-                if d:
-                    mid_sum[p, d] = value.astype(BF16)
-                    scatter2[p][d].start()
-                else:
-                    landed[p, 0] = value.astype(BF16)
-
-        early.wait_recv()
+                mid_sum[p, d] = value.astype(BF16)
+                scatter2[p][d].start()
+
+        @pl.when(turn == 0)
+        def _():
+            swap_ids.wait()
+
+        for copy in early:
+            copy.wait_recv()
         ahead, _, _, _ = routing(turn + 1)
-        next_route[...] = contract(ahead, early_in[PATHS * lanes :, 0:lanes], 1, 1).astype(BF16)
+        next_route[...] = contract(ahead, early_in[routes, 0:lanes], 1, 1).astype(BF16)
         for p in range(PATHS):
             next_pre[p] = jnp.dot(ahead, early_in[p * lanes : (p + 1) * lanes, :], preferred_element_type=F32)
 
         for p in range(PATHS):
-
-            @pl.when(turn > 0)
-            def _():
-                late[p].wait_send()
-
+            sent(terms.at[p, pl.ds(0, many)], rs1_send.at[p])
+        gate = gates_in[:, 0:1]
+        for p in range(PATHS):
+            came(landed.at[p], rs2_recv.at[p])
             result = landed[p, 0].astype(F32)
-            for d in reversed(order):
-                scatter2[p][d].wait_recv()
-                result = result + landed[p, side - d].astype(F32)
-            late_out[p] = (chosen[p].astype(F32) + gates[:, 0:1] * result).astype(BF16)
-            late[p].start()
-        for p in range(PATHS):
-            for copy in (*scatter1[p].values(), *scatter2[p].values()):
-                copy.wait_send()
-        for p in range(PATHS):
-            late[p].wait_recv()
-            picked = next_pre[p] + jnp.dot(next_route[...], late_in[p], preferred_element_type=F32)
+            for d in range(1, side):
+                result = result + landed[p, d].astype(F32)
+            value = (early_in[slots_at[p], :].astype(F32) + gate * result).astype(BF16)
+            fresh[p] = value
+            picked = next_pre[p] + jnp.dot(next_route[...], value, preferred_element_type=F32)
 
             @pl.when(turn < sections - 1)
             def _():
                 chosen[p] = picked.astype(BF16)
                 start_gather(p)
 
+        @pl.when(turn < sections - 1)
+        def _():
+            pl.semaphore_signal(credit_landed, inc=1, device_id=below, device_id_type=MESH)
+
+        for p in range(PATHS):
+            sent(mid_sum.at[p], rs2_send.at[p])
+
         return carry
 
     lax.fori_loop(0, sections, turn_body, 0)
@@ -387,9 +407,8 @@
         final = merged(p)
         for a in range(FOLD):
             out[0, :, columns(p, a)] = final[a * n_rows : (a + 1) * n_rows, :]
-    early.wait_send()
-    for p in range(PATHS):
-        late[p].wait_send()
+    for copy in early:
+        copy.wait_send()
 
 
 def body(sections, side, acts, norm_gain, router, w_gate, w_up, w_down, expert_ids):
@@ -415,10 +434,10 @@
             pltpu.VMEM(acts.shape, BF16),
             pltpu.VMEM(norm_gain.shape, F32),
             pltpu.VMEM(router.shape, BF16),
-            pltpu.VMEM(expert_ids.shape, jnp.int32),
+            pltpu.VMEM((2, *expert_ids.shape[1:]), jnp.int32),
             pltpu.VMEM((2, depth, hid), BF16),
             pltpu.VMEM((2, depth, hid), BF16),
-            pltpu.VMEM((2, hid, depth), BF16),
+            pltpu.VMEM((2 * hid, depth), BF16),
             pltpu.VMEM((PATHS, chips, block, width), BF16),
             pltpu.VMEM((PATHS, chips, block, width), BF16),
             pltpu.VMEM((PATHS, side, side, block, width), BF16),
@@ -426,29 +445,28 @@
             pltpu.VMEM((PATHS, side, block, width), BF16),
             pltpu.VMEM((PATHS, lanes, width), BF16),
             pltpu.VMEM((PATHS, block, width), BF16),
-            pltpu.VMEM((PATHS * lanes + block, width), BF16),
-            pltpu.VMEM((PATHS * lanes + block, width), BF16),
-            pltpu.VMEM((PATHS, block, width), BF16),
+            pltpu.VMEM((PATHS * (lanes + block) + block, width), BF16),
+            pltpu.VMEM((PATHS * (lanes + block) + block, width), BF16),
             pltpu.VMEM((PATHS, block, width), BF16),
             pltpu.VMEM((taken, part), BF16),
             pltpu.VMEM((taken, 4 * hid), F32),
-            pltpu.VMEM((total, 2 * FOLD * hid), BF16),
+            pltpu.VMEM((taken, 2 * hid), BF16),
+            pltpu.VMEM((total, width), BF16),
             pltpu.VMEM((total, total), BF16),
-            pltpu.VMEM((total, taken), BF16),
+            pltpu.VMEM((total, total), BF16),
             pltpu.VMEM((PATHS, block, width), F32),
             pltpu.VMEM((block, block), BF16),
             pltpu.VMEM((PATHS, block, width), F32),
             pltpu.VMEM((block, 128), F32),
-            dma((4,)), dma((5,)), dma((5,)), dma((5,)),
-            dma((PATHS, side - 1)), dma((PATHS, side - 1)),
-            dma((PATHS, side, side - 1)), dma((PATHS, side, side - 1)),
-            dma((PATHS, side, side - 1)), dma((PATHS, side, side - 1)),
-            dma((PATHS, side - 1)), dma((PATHS, side - 1)),
-            dma((PATHS + 1,)), dma((PATHS + 1,)),
-            pltpu.SemaphoreType.REGULAR,
+            pltpu.VMEM((block, 128), F32),
+            dma((4,)), dma((5,)), dma((6,)), dma((6,)),
+            dma((PATHS,)), dma((PATHS, side - 1)), dma((PATHS,)),
+            dma((PATHS,)), dma((PATHS, side)), dma((PATHS,)), dma((PATHS,)),
+            dma((2,)), dma((2,)),
+            pltpu.SemaphoreType.REGULAR, pltpu.SemaphoreType.REGULAR,
         ],
         compiler_params=pltpu.CompilerParams(
-            collective_id=0, has_side_effects=True, vmem_limit_bytes=60 * 2**20
+            collective_id=0, has_side_effects=True, vmem_limit_bytes=56 * 2**20
         ),
         name="relay",
     )(acts, norm_gain, router, w_gate, w_up, w_down, expert_ids)

time: 223 us -> 200 us (0.90); the launches traced: 222 us -> 197 us
  Pallas kernels: 221 us -> 195 us
    pallas_call x1, Pallas kernels: 221 us -> 195 us  [body(): pl.pallas_call(functools.partial(relay_kernel, sections, side), out_shape...]
where the time goes in v3:
time: 200 us; the launch traced here: 197 us
  Pallas kernels  195 us (98%)
    pallas_call x1, Pallas kernels, body(): pl.pallas_call(functools.partial(relay_kernel, sections, side), out_shape...  195 us

profile of v3, /device:TPU:6, one launch (start us, length us, event | category | flops | bytes accessed | tf_op | source)
XLA Modules:
  0.0 197.0 jit_solution(4423463796594309563)
XLA Ops:
  0.0 195.3 %relay.1 = bf16[1,16,6144]{2,1,0:T(8,128)(2,1)} custom-call(bf16[1,16,6144]{2,1,0:T(8,128)(2,1)} %acts_hbm.1, f32[1,6144]{1,0:T(1,128)} %gain_hbm.1, bf16[1,8,6144]{2,1,0:T(8,128)(2,1)} %bitcast.2, bf16[1,6144,256]{2,1,0:T(8,128)(2,1)} %w_gate.1, bf16[1,6144,256]{2,1,0:T(8,128)(2,1)} %w_up.1, bf16[1,256,6144]{2,1,0:T(8,128)(2,1)} %w_down.1, ...), custom_call_target="tpu_custom_call" | custom-call | tf_op jit(solution)/shard_map/relay/pallas_call | solution.py:428
  195.4 1.6 copy.9

commit v4 on v3

--- a/solution.py
+++ b/solution.py
@@ -33,7 +33,7 @@
     sections, side, acts_hbm, gain_hbm, router_hbm, w_gate, w_up, w_down, ids_hbm, out,
     acts, gain, router, ids,
     wg, wu, wd, gathered, terms, mid, mid_sum, landed, rows, chosen, early_out, early_in, fresh,
-    xg, sums_gu, hidden, stacked, perm, perm_back, gain_fold, next_route, next_pre, gates_out, gates_in,
+    sums_gu, perm, perm_back, gain_fold, next_route, next_pre, gates_out, gates_in,
     in_sem, w_local, w_send, w_recv, ag_send, ag1_recv, ag2_recv,
     rs1_send, rs1_recv, rs2_send, rs2_recv, z_send, z_recv, credit_early, credit_landed,
 ):
@@ -60,11 +60,9 @@
     def device_at(dx, dy):
         return (section, chip_at(dx, dy) * 2 + core)
 
-    def along(axis, d):
-        return (d, 0) if axis == 0 else (0, d)
-
-    def place(axis):
-        return cx if axis == 0 else cy
+    def steps(p, d, e=0):
+        turned = lax.rem(p + core, 2)
+        return d + turned * (e - d), e + turned * (d - e)
 
     order = far_first(side)
     sibling = (section, chip * 2 + 1 - core)
@@ -77,7 +75,7 @@
     partners = [sibling, above, below]
     for axis in range(2):
         for d in order:
-            there = chip_at(*along(axis, d)) * 2
+            there = chip_at(*((d, 0) if axis == 0 else (0, d))) * 2
             partners += [
                 (section, there + core), (next_section, there + 1 - core), (last_section, there + 1 - core)
             ]
@@ -151,14 +149,13 @@
         )
 
     def own_chip(p, d):
-        dx, dy = along(p, side - d)
-        return chip_at(dx, dy) if d else chip
+        return chip_at(*steps(p, side - d)) if d else chip
 
     gather1 = [
         {
             d: remote(
                 chosen.at[p], gathered.at[p, chip], ag_send.at[p], ag1_recv.at[p, d - 1],
-                device_at(*along(p, d)),
+                device_at(*steps(p, d)),
             )
             for d in order
         }
@@ -170,7 +167,7 @@
                 chosen.at[p] if d == 0 else gathered.at[p, own_chip(p, d)],
                 gathered.at[p, own_chip(p, d)],
                 ag_send.at[p], ag2_recv.at[p],
-                device_at(*along(1 - p, e)),
+                device_at(*steps(p, 0, e)),
             )
             for d in range(side)
             for e in order
@@ -180,10 +177,10 @@
     scatter1 = [
         {
             (d, e): remote(
-                terms.at[p, chip_at(*(d, e) if p == 0 else (e, d))],
+                terms.at[p, chip_at(*steps(p, d, e))],
                 mid.at[p, side - e, d],
                 rs1_send.at[p], rs1_recv.at[p, d],
-                device_at(*along(1 - p, e)),
+                device_at(*steps(p, 0, e)),
             )
             for d in range(side)
             for e in order
@@ -194,7 +191,7 @@
         {
             d: remote(
                 mid_sum.at[p, d], landed.at[p, (side - d) % side], rs2_send.at[p], rs2_recv.at[p],
-                (next_section, chip_at(*along(p, d)) * 2 + 1 - core),
+                (next_section, chip_at(*steps(p, d)) * 2 + 1 - core),
             )
             for d in range(side)
         }
@@ -308,12 +305,6 @@
         square = jnp.zeros((taken, 1), F32)
         for p in range(PATHS):
             came(gathered.at[p, pl.ds(0, many)], ag2_recv.at[p])
-            everyone = gathered[p].reshape(total, width)
-            ordered = jnp.dot(perm[...], everyone, preferred_element_type=F32)
-            for a in range(FOLD):
-                piece = ordered[a * taken : (a + 1) * taken, :]
-                square = square + jnp.sum(piece * piece, axis=1, keepdims=True)
-                xg[:, a * width : (a + 1) * width] = (piece * gain[0:1, columns(p, a)]).astype(BF16)
 
             @pl.when(turn == 0)
             def _():
@@ -321,19 +312,23 @@
                     loads[n].wait()
                     swaps[n].wait()
 
-            for half in range(2):
-                for n, w in ((0, wg), (1, wu)):
-                    dot = jnp.dot(xg[...], w[half, p * part : (p + 1) * part, :], preferred_element_type=F32)
-                    span = slice((2 * n + half) * hid, (2 * n + half + 1) * hid)
-                    if p == 0:
-                        sums_gu[:, span] = dot
-                    else:
-                        sums_gu[:, span] = sums_gu[:, span] + dot
+            everyone = gathered[p].reshape(total, width)
+            ordered = jnp.dot(perm[...], everyone, preferred_element_type=F32)
+            dots = [0.0] * 4
+            for a in range(FOLD):
+                piece = ordered[a * taken : (a + 1) * taken, :]
+                square = square + jnp.sum(piece * piece, axis=1, keepdims=True)
+                piece = (piece * gain[0:1, columns(p, a)]).astype(BF16)
+                for n, w in enumerate((wg.at[0], wg.at[1], wu.at[0], wu.at[1])):
+                    dots[n] = dots[n] + jnp.dot(piece, w[columns(p, a), :], preferred_element_type=F32)
+            if p == 0:
+                for n in range(4):
+                    sums_gu[:, n * hid : (n + 1) * hid] = dots[n]
         scale = lax.rsqrt(square / depth + EPS)
-        for half in range(2):
-            g = sums_gu[:, half * hid : (half + 1) * hid] * scale
-            u = sums_gu[:, (2 + half) * hid : (3 + half) * hid] * scale
-            hidden[:, half * hid : (half + 1) * hid] = (jax.nn.silu(g) * u).astype(BF16)
+        dots = [dots[n] + sums_gu[:, n * hid : (n + 1) * hid] for n in range(4)]
+        hidden = jnp.concatenate(
+            [(jax.nn.silu(dots[half] * scale) * (dots[2 + half] * scale)).astype(BF16) for half in range(2)], axis=1
+        )
 
         @pl.when(turn == 0)
         def _():
@@ -341,11 +336,14 @@
             swaps[4].wait()
 
         for p in range(PATHS):
-            for a in range(FOLD):
-                stacked[a * taken : (a + 1) * taken, :] = jnp.dot(
-                    hidden[...], wd[:, columns(p, a)], preferred_element_type=F32
-                ).astype(BF16)
-            reordered = jnp.dot(perm_back[...], stacked[...], preferred_element_type=F32)
+            stacked = jnp.concatenate(
+                [
+                    jnp.dot(hidden, wd[:, columns(p, a)], preferred_element_type=F32).astype(BF16)
+                    for a in range(FOLD)
+                ],
+                axis=0,
+            )
+            reordered = jnp.dot(perm_back[...], stacked, preferred_element_type=F32)
             terms[p] = reordered.astype(BF16).reshape(chips, block, width)
             if p == 0:
                 for q in range(PATHS):
@@ -354,36 +352,29 @@
                 for e in order:
                     scatter1[p][d, e].start()
 
-        for p in range(PATHS):
-            for d in (*order, 0):
-                here = chip_at(*along(p, d))
-                value = terms[p, here].astype(F32)
-                came(mid.at[p, 0, pl.ds(0, few)], rs1_recv.at[p, d])
-                for e in reversed(order):
-                    value = value + mid[p, side - e, d].astype(F32)
-                mid_sum[p, d] = value.astype(BF16)
-                scatter2[p][d].start()
-
-        @pl.when(turn == 0)
-        def _():
-            swap_ids.wait()
-
-        for copy in early:
-            copy.wait_recv()
-        ahead, _, _, _ = routing(turn + 1)
-        next_route[...] = contract(ahead, early_in[routes, 0:lanes], 1, 1).astype(BF16)
-        for p in range(PATHS):
-            next_pre[p] = jnp.dot(ahead, early_in[p * lanes : (p + 1) * lanes, :], preferred_element_type=F32)
-
-        for p in range(PATHS):
-            sent(terms.at[p, pl.ds(0, many)], rs1_send.at[p])
-        gate = gates_in[:, 0:1]
-        for p in range(PATHS):
+        def look_ahead():
+            for copy in early:
+                copy.wait_recv()
+            ahead, _, _, _ = routing(turn + 1)
+            next_route[...] = contract(ahead, early_in[routes, 0:lanes], 1, 1).astype(BF16)
+            for p in range(PATHS):
+                next_pre[p] = jnp.dot(ahead, early_in[p * lanes : (p + 1) * lanes, :], preferred_element_type=F32)
+
+        def pass_up(p, d):
+            here = chip_at(*steps(p, d))
+            value = terms[p, here].astype(F32)
+            came(mid.at[p, 0, pl.ds(0, few)], rs1_recv.at[p, d])
+            for e in reversed(order):
+                value = value + mid[p, side - e, d].astype(F32)
+            mid_sum[p, d] = value.astype(BF16)
+            scatter2[p][d].start()
+
+        def take_in(p):
             came(landed.at[p], rs2_recv.at[p])
             result = landed[p, 0].astype(F32)
             for d in range(1, side):
                 result = result + landed[p, d].astype(F32)
-            value = (early_in[slots_at[p], :].astype(F32) + gate * result).astype(BF16)
+            value = (early_in[slots_at[p], :].astype(F32) + gates_in[:, 0:1] * result).astype(BF16)
             fresh[p] = value
             picked = next_pre[p] + jnp.dot(next_route[...], value, preferred_element_type=F32)
 
@@ -392,11 +383,23 @@
                 chosen[p] = picked.astype(BF16)
                 start_gather(p)
 
+        @pl.when(turn == 0)
+        def _():
+            swap_ids.wait()
+
+        look_ahead()
+        for p in range(PATHS):
+            for d in (*order, 0):
+                pass_up(p, d)
+        for p in range(PATHS):
+            take_in(p)
+
         @pl.when(turn < sections - 1)
         def _():
             pl.semaphore_signal(credit_landed, inc=1, device_id=below, device_id_type=MESH)
 
         for p in range(PATHS):
+            sent(terms.at[p, pl.ds(0, many)], rs1_send.at[p])
             sent(mid_sum.at[p], rs2_send.at[p])
 
         return carry
@@ -448,10 +451,7 @@
             pltpu.VMEM((PATHS * (lanes + block) + block, width), BF16),
             pltpu.VMEM((PATHS * (lanes + block) + block, width), BF16),
             pltpu.VMEM((PATHS, block, width), BF16),
-            pltpu.VMEM((taken, part), BF16),
             pltpu.VMEM((taken, 4 * hid), F32),
-            pltpu.VMEM((taken, 2 * hid), BF16),
-            pltpu.VMEM((total, width), BF16),
             pltpu.VMEM((total, total), BF16),
             pltpu.VMEM((total, total), BF16),
             pltpu.VMEM((PATHS, block, width), F32),

time: 200 us -> 193 us (0.965)
  Pallas kernels: 195 us -> 190 us
    pallas_call x1, Pallas kernels: 195 us -> 190 us  [body(): pl.pallas_call(functools.partial(relay_kernel, sections, side), out_shape...]
where the time goes in v4:
time: 193 us; the launch traced here: 192 us
  Pallas kernels  190 us (98%)
    pallas_call x1, Pallas kernels, body(): pl.pallas_call(functools.partial(relay_kernel, sections, side), out_shape...  190 us

profile of v4, /device:TPU:6, one launch (start us, length us, event | category | flops | bytes accessed | tf_op | source)
XLA Modules:
  0.0 191.7 jit_solution(367081690161146552)
XLA Ops:
  0.0 190.1 %relay.1 = bf16[1,16,6144]{2,1,0:T(8,128)(2,1)} custom-call(bf16[1,16,6144]{2,1,0:T(8,128)(2,1)} %acts_hbm.1, f32[1,6144]{1,0:T(1,128)} %gain_hbm.1, bf16[1,8,6144]{2,1,0:T(8,128)(2,1)} %bitcast.2, bf16[1,6144,256]{2,1,0:T(8,128)(2,1)} %w_gate.1, bf16[1,6144,256]{2,1,0:T(8,128)(2,1)} %w_up.1, bf16[1,256,6144]{2,1,0:T(8,128)(2,1)} %w_down.1, ...), custom_call_target="tpu_custom_call" | custom-call | tf_op jit(solution)/shard_map/relay/pallas_call | solution.py:431
  190.1 1.6 copy.9

commit v5 on v4

--- a/solution.py
+++ b/solution.py
@@ -72,13 +72,14 @@
     below = (last_section, chip * 2 + 1 - core)
 
     barrier = pltpu.get_barrier_semaphore()
-    partners = [sibling, above, below]
+    partners = [sibling, above]
+    senders = [below]
     for axis in range(2):
         for d in order:
             there = chip_at(*((d, 0) if axis == 0 else (0, d))) * 2
-            partners += [
-                (section, there + core), (next_section, there + 1 - core), (last_section, there + 1 - core)
-            ]
+            partners += [(section, there + core), (next_section, there + 1 - core)]
+            senders.append((last_section, there + 1 - core))
+    partners += senders
     for device in partners:
         pl.semaphore_signal(barrier, inc=1, device_id=device, device_id_type=MESH)
 
@@ -95,7 +96,9 @@
         for src, dst in ((w_gate, wg), (w_up, wu)):
             span = pl.ds(p * part, part)
             pieces.append((src.at[0, span], dst.at[0, span], dst.at[1, span]))
-    pieces.append((w_down.at[0], wd.at[pl.ds(0, hid)], wd.at[pl.ds(hid, hid)]))
+    for p in range(PATHS):
+        span = pl.ds(p * part, part)
+        pieces.append((w_down.at[0, :, span], wd.at[pl.ds(0, hid), span], wd.at[pl.ds(hid, hid), span]))
     loads = [pltpu.make_async_copy(src, dst, w_local.at[i]) for i, (src, dst, _) in enumerate(pieces)]
     for load in loads:
         load.start()
@@ -197,10 +200,13 @@
         }
         for p in range(PATHS)
     ]
-    early = [
-        remote(early_out, early_in, z_send.at[0], z_recv.at[0], above),
-        remote(gates_out, gates_in, z_send.at[1], z_recv.at[1], above),
-    ]
+
+    def early(slot):
+        return [
+            remote(early_out, early_in.at[slot], z_send.at[0], z_recv.at[slot, 0], above),
+            remote(gates_out, gates_in.at[slot], z_send.at[1], z_recv.at[slot, 1], above),
+        ]
+
     swap_ids = remote(ids.at[0], ids.at[1], w_send.at[len(pieces)], w_recv.at[len(pieces)], sibling)
     few, many = side - 1, side * (side - 1)
 
@@ -222,9 +228,9 @@
     routes = slice(PATHS * lanes, PATHS * lanes + block)
     slots_at = [slice(routes.stop + p * block, routes.stop + (p + 1) * block) for p in range(PATHS)]
 
-    def merged(p):
-        incoming = contract(early_in[routes, 0:lanes], fresh[p], 0, 0)
-        return (early_in[p * lanes : (p + 1) * lanes, :].astype(F32) + incoming).astype(BF16)
+    def merged(slot, p):
+        incoming = contract(early_in[slot, routes, 0:lanes], fresh[p], 0, 0)
+        return (early_in[slot, p * lanes : (p + 1) * lanes, :].astype(F32) + incoming).astype(BF16)
 
     for p in range(PATHS):
         start_gather(p)
@@ -241,13 +247,9 @@
         gain_fold[p] = folded
 
     def turn_body(turn, carry):
-        for p in range(PATHS):
-            if p == PATHS - 1:
-
-                @pl.when(turn > 0)
-                def _():
-                    pl.semaphore_wait(credit_landed, 1)
-
+        now, before = lax.rem(turn, 2), lax.rem(turn + 1, 2)
+
+        for p in range(PATHS):
             for d in reversed(order):
                 gather1[p][d].wait_recv()
                 for e in order:
@@ -256,7 +258,12 @@
         @pl.when(turn > 0)
         def _():
             for p in range(PATHS):
-                rows[p] = merged(p)
+                rows[p] = merged(before, p)
+            for device in senders:
+                pl.semaphore_signal(credit_landed, inc=1, device_id=device, device_id_type=MESH)
+
+        @pl.when((turn > 0) & (turn < sections - 1))
+        def _():
             pl.semaphore_signal(credit_early, inc=1, device_id=below, device_id_type=MESH)
 
         select, rival, valid, keep = routing(turn)
@@ -284,7 +291,7 @@
 
         @pl.when(turn > 0)
         def _():
-            for copy in early:
+            for copy in early(before):
                 copy.wait_send()
 
         for p in range(PATHS):
@@ -295,11 +302,11 @@
         early_out[routes, 0:lanes] = select
         gates_out[...] = jnp.broadcast_to(gate, gates_out.shape)
 
-        @pl.when(turn > 0)
+        @pl.when(turn > 1)
         def _():
             pl.semaphore_wait(credit_early, 1)
 
-        for copy in early:
+        for copy in early(now):
             copy.start()
 
         square = jnp.zeros((taken, 1), F32)
@@ -330,12 +337,13 @@
             [(jax.nn.silu(dots[half] * scale) * (dots[2 + half] * scale)).astype(BF16) for half in range(2)], axis=1
         )
 
-        @pl.when(turn == 0)
-        def _():
-            loads[4].wait()
-            swaps[4].wait()
-
-        for p in range(PATHS):
+        for p in range(PATHS):
+
+            @pl.when(turn == 0)
+            def _():
+                loads[4 + p].wait()
+                swaps[4 + p].wait()
+
             stacked = jnp.concatenate(
                 [
                     jnp.dot(hidden, wd[:, columns(p, a)], preferred_element_type=F32).astype(BF16)
@@ -353,12 +361,13 @@
                     scatter1[p][d, e].start()
 
         def look_ahead():
-            for copy in early:
+            for copy in early(now):
                 copy.wait_recv()
             ahead, _, _, _ = routing(turn + 1)
-            next_route[...] = contract(ahead, early_in[routes, 0:lanes], 1, 1).astype(BF16)
+            next_route[...] = contract(ahead, early_in[now, routes, 0:lanes], 1, 1).astype(BF16)
             for p in range(PATHS):
-                next_pre[p] = jnp.dot(ahead, early_in[p * lanes : (p + 1) * lanes, :], preferred_element_type=F32)
+                held_over = early_in[now, p * lanes : (p + 1) * lanes, :]
+                next_pre[p] = jnp.dot(ahead, held_over, preferred_element_type=F32)
 
         def pass_up(p, d):
             here = chip_at(*steps(p, d))
@@ -374,7 +383,7 @@
             result = landed[p, 0].astype(F32)
             for d in range(1, side):
                 result = result + landed[p, d].astype(F32)
-            value = (early_in[slots_at[p], :].astype(F32) + gates_in[:, 0:1] * result).astype(BF16)
+            value = (early_in[now, slots_at[p], :].astype(F32) + gates_in[now, :, 0:1] * result).astype(BF16)
             fresh[p] = value
             picked = next_pre[p] + jnp.dot(next_route[...], value, preferred_element_type=F32)
 
@@ -387,16 +396,18 @@
         def _():
             swap_ids.wait()
 
-        look_ahead()
-        for p in range(PATHS):
-            for d in (*order, 0):
+        @pl.when(turn > 0)
+        def _():
+            pl.semaphore_wait(credit_landed, len(senders))
+
+        groups = (*order, 0)
+        for p in range(PATHS):
+            for n, d in enumerate(groups):
                 pass_up(p, d)
+                if p == 0 and n == 1:
+                    look_ahead()
         for p in range(PATHS):
             take_in(p)
-
-        @pl.when(turn < sections - 1)
-        def _():
-            pl.semaphore_signal(credit_landed, inc=1, device_id=below, device_id_type=MESH)
 
         for p in range(PATHS):
             sent(terms.at[p, pl.ds(0, many)], rs1_send.at[p])
@@ -407,10 +418,10 @@
     lax.fori_loop(0, sections, turn_body, 0)
 
     for p in range(PATHS):
-        final = merged(p)
+        final = merged((sections - 1) % 2, p)
         for a in range(FOLD):
             out[0, :, columns(p, a)] = final[a * n_rows : (a + 1) * n_rows, :]
-    for copy in early:
+    for copy in early((sections - 1) % 2):
         copy.wait_send()
 
 
@@ -449,7 +460,7 @@
             pltpu.VMEM((PATHS, lanes, width), BF16),
             pltpu.VMEM((PATHS, block, width), BF16),
             pltpu.VMEM((PATHS * (lanes + block) + block, width), BF16),
-            pltpu.VMEM((PATHS * (lanes + block) + block, width), BF16),
+            pltpu.VMEM((2, PATHS * (lanes + block) + block, width), BF16),
             pltpu.VMEM((PATHS, block, width), BF16),
             pltpu.VMEM((taken, 4 * hid), F32),
             pltpu.VMEM((total, total), BF16),
@@ -458,11 +469,11 @@
             pltpu.VMEM((block, block), BF16),
             pltpu.VMEM((PATHS, block, width), F32),
             pltpu.VMEM((block, 128), F32),
-            pltpu.VMEM((block, 128), F32),
-            dma((4,)), dma((5,)), dma((6,)), dma((6,)),
+            pltpu.VMEM((2, block, 128), F32),
+            dma((4,)), dma((6,)), dma((7,)), dma((7,)),
             dma((PATHS,)), dma((PATHS, side - 1)), dma((PATHS,)),
             dma((PATHS,)), dma((PATHS, side)), dma((PATHS,)), dma((PATHS,)),
-            dma((2,)), dma((2,)),
+            dma((2,)), dma((2, 2)),
             pltpu.SemaphoreType.REGULAR, pltpu.SemaphoreType.REGULAR,
         ],
         compiler_params=pltpu.CompilerParams(

time: 193 us -> 190 us (0.984)
  Pallas kernels: 190 us -> 186 us
    pallas_call x1, Pallas kernels: 190 us -> 186 us  [body(): pl.pallas_call(functools.partial(relay_kernel, sections, side), out_shape...]
where the time goes in v5:
time: 190 us; the launch traced here: 188 us
  Pallas kernels  186 us (98%)
    pallas_call x1, Pallas kernels, body(): pl.pallas_call(functools.partial(relay_kernel, sections, side), out_shape...  186 us

profile of v5, /device:TPU:6, one launch (start us, length us, event | category | flops | bytes accessed | tf_op | source)
XLA Modules:
  0.0 187.6 jit_solution(9388676851042074413)
XLA Ops:
  0.0 186.0 %relay.1 = bf16[1,16,6144]{2,1,0:T(8,128)(2,1)} custom-call(bf16[1,16,6144]{2,1,0:T(8,128)(2,1)} %acts_hbm.1, f32[1,6144]{1,0:T(1,128)} %gain_hbm.1, bf16[1,8,6144]{2,1,0:T(8,128)(2,1)} %bitcast.2, bf16[1,6144,256]{2,1,0:T(8,128)(2,1)} %w_gate.1, bf16[1,6144,256]{2,1,0:T(8,128)(2,1)} %w_up.1, bf16[1,256,6144]{2,1,0:T(8,128)(2,1)} %w_down.1, ...), custom_call_target="tpu_custom_call" | custom-call | tf_op jit(solution)/shard_map/relay/pallas_call | solution.py:442
  186.0 1.6 copy.9

commit v6 on v5

--- a/solution.py
+++ b/solution.py
@@ -252,7 +252,9 @@
         for p in range(PATHS):
             for d in reversed(order):
                 gather1[p][d].wait_recv()
-                for e in order:
+                gather2[p][d, order[0]].start()
+            for d in reversed(order):
+                for e in order[1:]:
                     gather2[p][d, e].start()
 
         @pl.when(turn > 0)

time: 190 us -> 191 us (level)
  no operation moved by 1% of the time
where the time goes in v6:
time: 191 us; the launch traced here: 189 us
  Pallas kernels  187 us (98%)
    pallas_call x1, Pallas kernels, body(): pl.pallas_call(functools.partial(relay_kernel, sections, side), out_shape...  187 us

profile of v6, /device:TPU:6, one launch (start us, length us, event | category | flops | bytes accessed | tf_op | source)
XLA Modules:
  0.0 189.0 jit_solution(18221345938123617971)
XLA Ops:
  0.0 187.4 %relay.1 = bf16[1,16,6144]{2,1,0:T(8,128)(2,1)} custom-call(bf16[1,16,6144]{2,1,0:T(8,128)(2,1)} %acts_hbm.1, f32[1,6144]{1,0:T(1,128)} %gain_hbm.1, bf16[1,8,6144]{2,1,0:T(8,128)(2,1)} %bitcast.2, bf16[1,6144,256]{2,1,0:T(8,128)(2,1)} %w_gate.1, bf16[1,6144,256]{2,1,0:T(8,128)(2,1)} %w_up.1, bf16[1,256,6144]{2,1,0:T(8,128)(2,1)} %w_down.1, ...), custom_call_target="tpu_custom_call" | custom-call | tf_op jit(solution)/shard_map/relay/pallas_call | solution.py:444
  187.4 1.6 copy.9

commit v7 on v5

--- a/solution.py
+++ b/solution.py
@@ -232,11 +232,11 @@
         incoming = contract(early_in[slot, routes, 0:lanes], fresh[p], 0, 0)
         return (early_in[slot, p * lanes : (p + 1) * lanes, :].astype(F32) + incoming).astype(BF16)
 
-    for p in range(PATHS):
-        start_gather(p)
     swap_ids.start()
     for swap in swaps:
         swap.start()
+    for p in range(PATHS):
+        start_gather(p)
 
     inputs[2].wait()
     inputs[3].wait()
@@ -356,9 +356,13 @@
             if p == 0:
                 for q in range(PATHS):
                     sent(gathered.at[q, pl.ds(0, few + many)], ag_send.at[q])
-            for d in (*order, 0):
+            if p == 0:
+                turns = [(0, d) for d in order[:2]]
+            else:
+                turns = [(1, order[0]), (0, order[2]) if few > 2 else (0, 0), (1, order[-2]), (0, 0), (1, order[-1]), (1, 0)]
+            for q, d in turns:
                 for e in order:
-                    scatter1[p][d, e].start()
+                    scatter1[q][d, e].start()
 
         def look_ahead():
             for copy in early(now):

time: 190 us -> 191 us (level)
  Pallas kernels: 186 us -> 189 us
    pallas_call x1, Pallas kernels: 186 us -> 189 us  [body(): pl.pallas_call(functools.partial(relay_kernel, sections, side), out_shape...]
where the time goes in v7:
time: 191 us; the launch traced here: 190 us
  Pallas kernels  189 us (99%)
    pallas_call x1, Pallas kernels, body(): pl.pallas_call(functools.partial(relay_kernel, sections, side), out_shape...  189 us

profile of v7, /device:TPU:6, one launch (start us, length us, event | category | flops | bytes accessed | tf_op | source)
XLA Modules:
  0.0 190.3 jit_solution(15953940518177036639)
XLA Ops:
  0.0 188.7 %relay.1 = bf16[1,16,6144]{2,1,0:T(8,128)(2,1)} custom-call(bf16[1,16,6144]{2,1,0:T(8,128)(2,1)} %acts_hbm.1, f32[1,6144]{1,0:T(1,128)} %gain_hbm.1, bf16[1,8,6144]{2,1,0:T(8,128)(2,1)} %bitcast.2, bf16[1,6144,256]{2,1,0:T(8,128)(2,1)} %w_gate.1, bf16[1,6144,256]{2,1,0:T(8,128)(2,1)} %w_up.1, bf16[1,256,6144]{2,1,0:T(8,128)(2,1)} %w_down.1, ...), custom_call_target="tpu_custom_call" | custom-call | tf_op jit(solution)/shard_map/relay/pallas_call | solution.py:446
  188.7 1.6 copy.9
